TPU v7x, 32 devices: a whole 2x2x4 slice. The times are simulated.
32 devices in a mesh: dp: 2 (over x), expert: 4 (over z), hidden: 4 (over y, core).
Axes of the slice: x: 2, y: 2, z: 4, core: 2. Of those that a mesh axis runs over, the one named last changes fastest.
Arguments:
- tokens: bfloat16 [16384, 1152], P(('dp', 'expert', 'hidden')), may hold values from -6 to 6
- route: int32 [16384, 1], P(('dp', 'expert', 'hidden')), may hold values from 0 to 3; in each aligned block of 512 rows (0 to 511, 512 to 1023, ...) at most 256 rows name the same one
- norm_gain: bfloat16 [1152], replicated, may hold values from 0.5 to 1.5
- router_weight: bfloat16 [1152, 4], replicated, may hold values from -0.119628906 to 0.119628906
- w_in: bfloat16 [4, 1152, 3072], P('expert', None, 'hidden'), may hold values from -0.1875 to 0.1875
- w_out: bfloat16 [4, 3072, 1152], P('expert', 'hidden'), may hold values from -0.8984375 to 0.8984375
- cotangent: bfloat16 [16384, 1152], P(('dp', 'expert', 'hidden')), may hold values from -6 to 6
Outputs:
- activations: bfloat16 [16384, 1152], P(('dp', 'expert', 'hidden'))
- input_grad: float32 [16384, 1152], P(('dp', 'expert', 'hidden'))
- gain_grad: float32 [1152], replicated
- router_grad: float32 [1152, 4], replicated
- w_in_grad: float32 [4, 1152, 3072], P('expert', None, 'hidden')
- w_out_grad: float32 [4, 3072, 1152], P('expert', 'hidden')
Inputs may be any that keep to these rules, and one draw needn't show every extreme that they name: `route`: in the rows of one device (aligned blocks of 512 rows) no expert is named more than 256 times, a bound that some block reaches; every expert is named somewhere.
All inputs are finite; a program needn't handle non-finite values.
Results may differ from a plain program's by a relative error of at most 0.0068.
Values may be sent and summed in bfloat16 or wider, within the bound.
A program may use at most 192 MiB of HBM per device.

v0:
```python
import jax
import jax.numpy as jnp
from jax import lax
from jax.sharding import PartitionSpec as P

HIGHEST = lax.Precision.HIGHEST
EPSILON = 1e-05


def activate(values):
    return jax.nn.gelu(values, approximate=True)


def on_device(tokens, route, norm_gain, router_weight, w_in, w_out, cotangent):
    inputs = tokens.astype(jnp.float32)
    row_count, width = inputs.shape
    expert_count = lax.axis_size("expert")
    hidden_count = lax.axis_size("hidden")
    capacity = 2 * row_count // expert_count
    chosen = route[:, 0]
    onehot_int = (chosen[:, None] == jnp.arange(expert_count, dtype=jnp.int32)[None, :]).astype(
        jnp.int32
    )
    within = jnp.sum((jnp.cumsum(onehot_int, axis=0) - 1) * onehot_int, axis=1)
    target = chosen * capacity + within
    onehot = onehot_int.astype(jnp.float32)
    gain_f32 = norm_gain.astype(jnp.float32)
    inverse = lax.rsqrt(jnp.mean(inputs * inputs, axis=1, keepdims=True) + EPSILON)
    normed_low = (inputs * inverse * gain_f32[None, :]).astype(jnp.bfloat16)
    logits = jnp.dot(normed_low, router_weight, preferred_element_type=jnp.float32)
    softmax_out = jax.nn.softmax(logits, axis=1)
    gate_value = jnp.sum(softmax_out * onehot, axis=1, keepdims=True)
    first_weight = w_in[0]
    second_weight = w_out[0]

    def bucket(values):
        empty = jnp.zeros((expert_count * capacity, width), values.dtype)
        return empty.at[target].set(values).reshape(expert_count, capacity, width)

    def unbucket(buckets):
        return buckets.reshape(expert_count * capacity, width)[target]

    def send_rows(buckets, backward):
        copies = jnp.repeat(buckets, hidden_count, axis=0)
        if backward:
            arrived = lax.all_to_all(
                copies, ("expert", "hidden"), split_axis=0, concat_axis=0, tiled=True
            )
        else:
            arrived = lax.all_to_all(
                copies, ("expert", "hidden"), split_axis=0, concat_axis=0, tiled=True
            )
        return arrived.reshape(-1, width)

    def return_rows(partial_out, backward):
        shaped = partial_out.reshape(expert_count * hidden_count, capacity, width)
        if backward:
            returned = lax.all_to_all(
                shaped, ("expert", "hidden"), split_axis=0, concat_axis=0, tiled=True
            )
        else:
            returned = lax.all_to_all(
                shaped, ("expert", "hidden"), split_axis=0, concat_axis=0, tiled=True
            )
        summed = jnp.sum(returned.reshape(expert_count, hidden_count, capacity, width), axis=1)
        return summed.astype(jnp.bfloat16)

    expert_in = send_rows(bucket(normed_low), False)
    hidden_pre = jnp.dot(expert_in, first_weight, preferred_element_type=jnp.float32)
    hidden_low = activate(hidden_pre).astype(jnp.bfloat16)
    partial_out = jnp.dot(hidden_low, second_weight, preferred_element_type=jnp.float32)
    expert_out = unbucket(return_rows(partial_out, False)).astype(jnp.float32)
    activations = (inputs + gate_value * expert_out).astype(jnp.bfloat16)
    upstream = cotangent.astype(jnp.float32)
    gate_grad = jnp.sum(upstream * expert_out, axis=1, keepdims=True)
    out_grad = (gate_value * upstream).astype(jnp.bfloat16)
    logit_grad = gate_grad * gate_value * (onehot - softmax_out)
    router_f32 = router_weight.astype(jnp.float32)
    router_part = jnp.dot(normed_low.astype(jnp.float32).T, logit_grad, precision=HIGHEST)
    normed_router = jnp.dot(logit_grad, router_f32.T, precision=HIGHEST)
    grad_rows = send_rows(bucket(out_grad), True)
    hidden_grad = jnp.dot(grad_rows, second_weight.T, preferred_element_type=jnp.float32)
    unused, pullback = jax.vjp(activate, hidden_pre)
    pre_grad = pullback(hidden_grad)[0].astype(jnp.bfloat16)
    second_grad = jnp.dot(hidden_low.T, grad_rows, preferred_element_type=jnp.float32)
    first_grad = jnp.dot(expert_in.T, pre_grad, preferred_element_type=jnp.float32)
    input_part = jnp.dot(pre_grad, first_weight.T, preferred_element_type=jnp.float32)
    expert_grad = unbucket(return_rows(input_part, True)).astype(jnp.float32)
    first_grad, second_grad = lax.psum((first_grad, second_grad), "dp")
    normed_grad = expert_grad + normed_router
    scaled = gain_f32[None, :] * normed_grad
    gain_part = jnp.sum(normed_grad * inputs * inverse, axis=0)
    cubed = inverse * inverse * inverse
    input_grad = (
        upstream
        + inverse * scaled
        - inputs * cubed * jnp.sum(scaled * inputs, axis=1, keepdims=True) / width
    )
    gain_grad, router_grad = lax.psum((gain_part, router_part), ("dp", "expert", "hidden"))
    return (activations, input_grad, gain_grad, router_grad, first_grad[None], second_grad[None])


def solution(mesh):
    placed = (
        P(("dp", "expert", "hidden"), None),
        P(("dp", "expert", "hidden"), None),
        P(),
        P(),
        P("expert", None, "hidden"),
        P("expert", "hidden", None),
        P(("dp", "expert", "hidden"), None),
    )
    return jax.shard_map(
        on_device,
        mesh=mesh,
        in_specs=placed,
        out_specs=(
            P(("dp", "expert", "hidden"), None),
            P(("dp", "expert", "hidden"), None),
            P(),
            P(),
            P("expert", None, "hidden"),
            P("expert", "hidden", None),
        ),
        check_vma=False,
    )
```

profile of v0, /device:TPU:0, one launch (start us, length us, event | category | flops | bytes accessed | tf_op | source)
XLA Modules:
  0.0 1401.8 jit_solution(16101656225142207865)
XLA Ops:
  7.2 1.7 fusion.10
  13.9 5.1 scatter_custom_fusion
  19.1 6.6 broadcast_in_dim.8
  25.7 7.6 all-to-all-start
  33.3 1.9 fusion.51
  35.3 4.4 scatter_custom_fusion.1
  39.6 162.6 %all-to-all-done = bf16[16,256,1152]{2,1,0:T(8,128)(2,1)} async-done(((bf16[16,256,1152]{2,1,0:T(8,128)(2,1)}), bf16[16,256,1152]{2,1,0:T(8,128)(2,1)}, u32[]{:S(2)}, u32[]{:S(2)}) %all-to-all-start) | async-done | bytes 9437216 | tf_op jit(solution)/shard_map/all_to_all | solution.py:50
  202.2 6.5 broadcast_in_dim.9
  208.8 41.0 %all-to-all-start.2 = ((bf16[16,256,1152]{2,1,0:T(8,128)(2,1)}), bf16[16,256,1152]{2,1,0:T(8,128)(2,1)}, u32[]{:S(2)}, u32[]{:S(2)}) async-start(bf16[16,256,1152]{2,1,0:T(8,128)(2,1)} %bitcast.66), calls=%async_computation.2 | async-start | bytes 18874368 | tf_op jit(solution)/shard_map/all_to_all | solution.py:46
  249.8 17.2 %multiply_convert_fusion = (bf16[4096,768]{1,0:T(8,128)(2,1)}, f32[4096,768]{1,0:T(8,128)}) fusion(bf16[4096,1152]{1,0:T(8,128)(2,1)} %bitcast.7, bf16[1,1152,768]{2,1,0:T(8,128)(2,1)S(1)} %copy-done), kind=kOutput, calls=%fused_computation.15 | convolution fusion | flops 7276068864 | bytes 30081024 | tf_op jit(solution)/shard_map/dot_general | solution.py:69
  267.0 151.8 %all-to-all-done.2 = bf16[16,256,1152]{2,1,0:T(8,128)(2,1)} async-done(((bf16[16,256,1152]{2,1,0:T(8,128)(2,1)}), bf16[16,256,1152]{2,1,0:T(8,128)(2,1)}, u32[]{:S(2)}, u32[]{:S(2)}) %all-to-all-start.2) | async-done | bytes 9437216 | tf_op jit(solution)/shard_map/all_to_all | solution.py:46
  418.8 19.7 %fusion.6 = bf16[4096,768]{1,0:T(8,128)(2,1)S(1)} fusion(f32[4096,768]{1,0:T(8,128)} %get-tuple-element.19, bf16[4096,1152]{1,0:T(8,128)(2,1)} %bitcast.16, bf16[1,768,1152]{2,1,0:T(8,128)(2,1)} %param.12), kind=kOutput, calls=%fused_computation.14 | convolution fusion | flops 7310671872 | bytes 30081024 | tf_op jit(solution)/shard_map/dot_general | solution.py:82
  438.5 2.6 copy-done.19
  441.1 23.1 %fusion.19 = f32[16,256,1152]{2,1,0:T(8,128)} fusion(bf16[16,256,768]{2,1,0:T(8,128)(2,1)S(1)} %bitcast.80, bf16[1,1152,768]{2,1,0:T(8,128)(2,1)S(1)} %copy-done), kind=kOutput, calls=%fused_computation.41 | convolution fusion | flops 7247757312 | bytes 26935296 | tf_op jit(solution)/shard_map/dot_general | solution.py:87
  464.2 40.9 %all-to-all-start.3 = ((f32[16,256,1152]{2,1,0:T(8,128)}), f32[16,256,1152]{2,1,0:T(8,128)}, u32[]{:S(2)}, u32[]{:S(2)}) async-start(f32[16,256,1152]{2,1,0:T(8,128)} %fusion.19), calls=%async_computation.3 | async-start | bytes 37748736 | tf_op jit(solution)/shard_map/all_to_all | solution.py:58
  505.1 14.1 %fusion.21 = f32[16,256,1152]{2,1,0:T(8,128)} fusion(bf16[16,256,768]{2,1,0:T(8,128)(2,1)} %bitcast.79, bf16[1,768,1152]{2,1,0:T(8,128)(2,1)S(1)} %copy-done.16), kind=kOutput, calls=%fused_computation.43 | convolution fusion | flops 7247757312 | bytes 26935296 | tf_op jit(solution)/shard_map/dot_general | solution.py:71
  519.2 319.2 %all-to-all-done.3 = f32[16,256,1152]{2,1,0:T(8,128)} async-done(((f32[16,256,1152]{2,1,0:T(8,128)}), f32[16,256,1152]{2,1,0:T(8,128)}, u32[]{:S(2)}, u32[]{:S(2)}) %all-to-all-start.3) | async-done | bytes 18874400 | tf_op jit(solution)/shard_map/all_to_all | solution.py:58
  838.4 78.7 %all-to-all-start.1 = ((f32[16,256,1152]{2,1,0:T(8,128)}), f32[16,256,1152]{2,1,0:T(8,128)}, u32[]{:S(2)}, u32[]{:S(2)}) async-start(f32[16,256,1152]{2,1,0:T(8,128)} %fusion.21), calls=%async_computation.1 | async-start | bytes 37748736 | tf_op jit(solution)/shard_map/all_to_all | solution.py:62
  917.1 13.7 convolution_bitcast_fusion
  930.8 12.9 convolution_bitcast_fusion.1
  944.4 8.1 bitcast_reduce_fusion
  952.5 3.0 gather_fusion.1
  955.5 294.9 %all-to-all-done.1 = f32[16,256,1152]{2,1,0:T(8,128)} async-done(((f32[16,256,1152]{2,1,0:T(8,128)}), f32[16,256,1152]{2,1,0:T(8,128)}, u32[]{:S(2)}, u32[]{:S(2)}) %all-to-all-start.1) | async-done | bytes 18874400 | tf_op jit(solution)/shard_map/all_to_all | solution.py:62
  1250.4 7.5 bitcast_reduce_fusion.1
  1257.9 3.2 gather_fusion
  1261.2 1.8 fusion.8
  1263.0 2.1 fusion.40
  1265.1 3.9 fusion.18
  1268.9 115.2 %all-reduce = (f32[1152]{0:T(1024)}, f32[1152,4]{0,1:T(4,128)}) all-reduce(f32[1152]{0:T(1024)} %get-tuple-element.6, f32[1152,4]{0,1:T(4,128)} %fusion.40), channel_id=1, replica_groups=mesh['dp'=2,'expert'=4,'hidden'=4] {'dp','expert','hidden'}, use_global_device_ids=true, to_apply=%region_14.15 | all-reduce | flops 5760 | bytes 46080 | tf_op jit(solution)/shard_map/psum | solution.py:99
  1384.1 4.6 fusion.9
  1388.7 4.2 copy.17
  1392.9 1.8 copy.18
  (55 shorter events, 5.9 us)
Async XLA Ops:
  7.2 242.6 %copy-start = (bf16[1,1152,768]{2,1,0:T(8,128)(2,1)S(1)}, bf16[1,1152,768]{2,1,0:T(8,128)(2,1)}, u32[]{:S(2)}) copy-start(bf16[1,1152,768]{2,1,0:T(8,128)(2,1)} %param.11) | copy-start | bytes 5308420
  9.5 23.8 %copy-start.10 = (f32[512]{0:T(512)}, f32[512]{0:T(512)S(1)}, u32[]{:S(2)}) copy-start(f32[512]{0:T(512)S(1)} %get-tuple-element.15) | copy-start | bytes 6148
  25.7 7.6 copy-start.17
  25.7 9.5 copy-start.9
  25.7 176.5 %all-to-all-start = ((bf16[16,256,1152]{2,1,0:T(8,128)(2,1)}), bf16[16,256,1152]{2,1,0:T(8,128)(2,1)}, u32[]{:S(2)}, u32[]{:S(2)}) async-start(bf16[16,256,1152]{2,1,0:T(8,128)(2,1)} %bitcast.65), calls=%async_computation | async-start | bytes 18874368 | tf_op jit(solution)/shard_map/all_to_all | solution.py:50
  33.3 2.0 copy-start.2
  35.1 173.6 %copy-start.7 = (f32[512,4]{0,1:T(4,128)}, f32[512,4]{0,1:T(4,128)S(1)}, u32[]{:S(2)}) copy-start(f32[512,4]{0,1:T(4,128)S(1)} %get-tuple-element.17) | copy-start | bytes 24580
  35.2 173.6 %copy-start.12 = (f32[512]{0:T(512)}, f32[512]{0:T(512)S(1)}, u32[]{:S(2)}) copy-start(f32[512]{0:T(512)S(1)} %get-tuple-element.16) | copy-start | bytes 6148
  35.2 173.6 %copy-start.14 = (f32[512]{0:T(512)}, f32[512]{0:T(512)S(1)}, u32[]{:S(2)}) copy-start(f32[512]{0:T(512)S(1)} %fusion.39) | copy-start | bytes 6148
  208.8 210.0 %all-to-all-start.2 = ((bf16[16,256,1152]{2,1,0:T(8,128)(2,1)}), bf16[16,256,1152]{2,1,0:T(8,128)(2,1)}, u32[]{:S(2)}, u32[]{:S(2)}) async-start(bf16[16,256,1152]{2,1,0:T(8,128)(2,1)} %bitcast.66), calls=%async_computation.2 | async-start | bytes 18874368 | tf_op jit(solution)/shard_map/all_to_all | solution.py:46
  438.5 2.6 copy-start.19
  464.2 40.9 %copy-start.16 = (bf16[1,768,1152]{2,1,0:T(8,128)(2,1)S(1)}, bf16[1,768,1152]{2,1,0:T(8,128)(2,1)}, u32[]{:S(2)}) copy-start(bf16[1,768,1152]{2,1,0:T(8,128)(2,1)} %param.12) | copy-start | bytes 5308420
  464.2 374.2 %all-to-all-start.3 = ((f32[16,256,1152]{2,1,0:T(8,128)}), f32[16,256,1152]{2,1,0:T(8,128)}, u32[]{:S(2)}, u32[]{:S(2)}) async-start(f32[16,256,1152]{2,1,0:T(8,128)} %fusion.19), calls=%async_computation.3 | async-start | bytes 37748736 | tf_op jit(solution)/shard_map/all_to_all | solution.py:58
  838.4 412.0 %all-to-all-start.1 = ((f32[16,256,1152]{2,1,0:T(8,128)}), f32[16,256,1152]{2,1,0:T(8,128)}, u32[]{:S(2)}, u32[]{:S(2)}) async-start(f32[16,256,1152]{2,1,0:T(8,128)} %fusion.21), calls=%async_computation.1 | async-start | bytes 37748736 | tf_op jit(solution)/shard_map/all_to_all | solution.py:62
  917.1 471.6 %all-reduce.4.cloned.1.call-start = ((), (), s32[]{:S(2)}) async-start(), calls=%async_computation.4 | async-start | bytes 14155776 | tf_op jit(solution)/shard_map/psum | solution.py:89
  1261.1 1.9 copy-start.3
  1261.1 1.9 copy-start.8
  1261.1 3.9 copy-start.6
  1261.1 3.9 copy-start.11
  1261.1 3.9 copy-start.13
  1261.1 3.9 copy-start.15
  1261.1 3.9 copy-start.18
  1265.1 119.1 %copy-start.4 = (bf16[512,1152]{1,0:T(8,128)(2,1)S(1)}, bf16[512,1152]{1,0:T(8,128)(2,1)}, u32[]{:S(2)}) copy-start(bf16[512,1152]{1,0:T(8,128)(2,1)} %gather_fusion) | copy-start | bytes 3538948
  1388.7 4.2 copy-start.5
  1388.7 6.0 copy-start.1
Sparse Core Ops, SparseCore 0:
  943.9 171.7 all-reduce.3
where the time goes:
time: 1400 us
  waiting for transfers between devices  928 us (66%)
  starting transfers between devices  168 us (12%)
  blocking collectives  115 us (8%)
  matrix products  109 us (8%)
  other arithmetic  38.7 us (3%)
  local copies, waits for them, and re-layouts  28.2 us (2%)
  between operations  14.6 us (1%)
    all_to_all x2, waiting for transfers between devices, return_rows(): lax.all_to_all(shaped, ('expert', 'hidden'), split_axis=0, concat_axis=0,...  614 us
    all_to_all x2, waiting for transfers between devices, send_rows(): lax.all_to_all(copies, ('expert', 'hidden'), split_axis=0, concat_axis=0,...  314 us
    all_to_all x2, starting transfers between devices, return_rows(): lax.all_to_all(shaped, ('expert', 'hidden'), split_axis=0, concat_axis=0,...  120 us
    psum x1, blocking collectives, on_device(): lax.psum((gain_part, router_part), ('dp', 'expert', 'hidden'))  115 us
    all_to_all x2, starting transfers between devices, send_rows(): lax.all_to_all(copies, ('expert', 'hidden'), split_axis=0, concat_axis=0,...  48.6 us
  transfers between devices with their start and end apart: 5, of which 4 were waited for; matrix products, arithmetic and copies ran while one was open for 7% of the time, Pallas kernels for 0%

commit v1 on v0

v1 whole, which is shorter than its diff:
```python
import functools

import jax
import jax.numpy as jnp
from jax import lax
from jax.experimental import pallas as pl
from jax.experimental.pallas import tpu as pltpu
from jax.sharding import PartitionSpec as P

HIGHEST = lax.Precision.HIGHEST
MESH = pl.DeviceIdType.MESH
EPSILON = 1e-05
F32 = jnp.float32
BF16 = jnp.bfloat16
AXES = ("dp", "expert", "hidden")
C0 = 0.7978845608
C1 = 0.044715


def flip(index, mask):
    out, bit = index, 1
    while bit <= mask:
        if mask & bit:
            out = out + bit - 2 * bit * lax.rem(lax.div(index, bit), 2)
        bit *= 2
    return out


def dot_nn(a, b):
    return lax.dot_general(a, b, (((1,), (0,)), ((), ())), preferred_element_type=F32)


def dot_nt(a, b):
    return lax.dot_general(a, b, (((1,), (1,)), ((), ())), preferred_element_type=F32)


def dot_tn(a, b):
    return lax.dot_general(a, b, (((0,), (0,)), ((), ())), preferred_element_type=F32)


def block_kernel(
    experts, pairs, order, hidden_tile, weight_parts, grad_parts,
    x_ref, route_ref, gain_ref, router_ref, win_ref, wout_ref, cot_ref,
    act_ref, ig_ref, red_ref, ga_in, ga_out, gb_in, gb_out, back_n, back_g,
    normed, place, inv, gate, probs, bn, bg, xs, gs, hs, ps, wp_in, wp_out, y_in, y_out,
    rs_send, rs_n, rs_g, own_n, own_g, total, red_in,
    w_send, w_recv, wf_send, wf_recv, z_send, z_recv, f_send, f_recv, r_send, r_recv,
    b_send, b_recv, y_send, y_recv, d_send, d_recv, red_send, red_recv, local,
):
    tokens, width = x_ref.shape
    hid = win_ref.shape[1]
    cap = bn.shape[0] // experts
    dp, z, h = (lax.axis_index(a) for a in AXES)
    c = lax.rem(h, 2)
    parity = lax.rem(dp, 2)
    core_peer = (dp, z, flip(h, 1))
    y_peer = (dp, z, flip(h, 2))
    x_peer = (flip(dp, 1), z, h)

    def remote(src, dst, send, recv, peer):
        return pltpu.make_async_remote_copy(
            src_ref=src, dst_ref=dst, send_sem=send, recv_sem=recv, device_id=peer, device_id_type=MESH
        )

    dp_steps = [1 << s for s in range(8) if (1 << s) < pairs]
    peers = [core_peer, y_peer] + [(flip(dp, m), z, h) for m in dp_steps]
    peers += [(dp, flip(z, k), h) for k in range(1, experts)]
    barrier = pltpu.get_barrier_semaphore()
    for peer in peers:
        pl.semaphore_signal(barrier, inc=1, device_id=peer, device_id_type=MESH)
    pl.semaphore_wait(barrier, len(peers))

    mats = ((win_ref, wp_in), (wout_ref, wp_out))

    def weight_copy(which, part):
        src, dst = mats[which]
        rows = src.shape[0] // weight_parts
        span = pl.ds(part * rows, rows)
        return remote(src.at[span], dst.at[span], w_send.at[part], w_recv.at[part], y_peer)

    def weight_pass(which, part):
        dst = mats[which][1]
        rows = dst.shape[0] // weight_parts
        span = pl.ds(part * rows, rows)
        return remote(dst.at[span], dst.at[span], wf_send.at[part], wf_recv.at[part], x_peer)

    for which in (0, 1):
        @pl.when(parity == which)
        def _():
            for part in range(weight_parts):
                weight_copy(which, part).start()

    tile = 128
    lane_e = lax.broadcasted_iota(jnp.int32, (tokens, experts), 1)
    onehot = (route_ref[...] == lane_e).astype(BF16)

    @pl.loop(0, tokens // tile)
    def _(i):
        rows = pl.ds(pl.multiple_of(i * tile, tile), tile)
        x = x_ref[rows, :].astype(F32)
        inverse = lax.rsqrt(jnp.mean(x * x, axis=1, keepdims=True) + EPSILON)
        low = (x * inverse * gain_ref[...].astype(F32)).astype(BF16)
        normed[rows, :] = low
        inv[rows, :] = inverse
        logits = dot_nn(low, router_ref[...])
        shifted = jnp.exp(logits - jnp.max(logits, axis=1, keepdims=True))
        soft = shifted / jnp.sum(shifted, axis=1, keepdims=True)
        probs[rows, :] = soft
        chosen = route_ref[rows, :]
        hot = (chosen == lax.broadcasted_iota(jnp.int32, (tile, experts), 1)).astype(F32)
        gate[rows, :] = jnp.sum(soft * hot, axis=1, keepdims=True)
        before = (
            lax.broadcasted_iota(jnp.int32, (tile, tokens), 1)
            < lax.broadcasted_iota(jnp.int32, (tile, tokens), 0) + i * tile
        ).astype(BF16)
        rank = jnp.sum(dot_nn(before, onehot) * hot, axis=1, keepdims=True)
        slot = chosen * cap + rank.astype(jnp.int32)
        place[rows, :] = (
            slot == lax.broadcasted_iota(jnp.int32, (tile, experts * cap), 1)
        ).astype(BF16)

    out_g = (gate[...] * cot_ref[...].astype(F32)).astype(BF16)

    def slots(e):
        return pl.ds(pl.multiple_of(e * cap, cap), cap)

    def arrive(source, core):
        return pl.ds(pl.multiple_of((source * 2 + core) * cap, cap), cap)

    def z_copy(t, k):
        src, dst = ((bn, xs), (bg, gs))[t]
        e = flip(z, k)
        return remote(
            src.at[slots(e)], dst.at[arrive(z, c)], z_send.at[t, k], z_recv.at[t, k], (dp, e, h)
        )

    def pair_copy(t, k):
        buf = (xs, gs)[t]
        span = arrive(flip(z, k), c)
        return remote(buf.at[span], buf.at[span], f_send.at[t, k], f_recv.at[t, k], core_peer)

    for k in order:
        e = flip(z, k)
        pick = place[:, slots(e)]
        if k == 0:
            xs[arrive(z, c), :] = dot_tn(pick, normed[...]).astype(BF16)
            gs[arrive(z, c), :] = dot_tn(pick, out_g).astype(BF16)
            for t in (0, 1):
                pair_copy(t, 0).start()
        else:
            bn[slots(e), :] = dot_tn(pick, normed[...]).astype(BF16)
            z_copy(0, k).start()
            bg[slots(e), :] = dot_tn(pick, out_g).astype(BF16)
            z_copy(1, k).start()

    for which in (0, 1):
        @pl.when(parity == which)
        def _():
            for part in range(weight_parts):
                weight_copy(which, part).wait_recv()
                weight_pass(which, part).start()
            for part in range(weight_parts):
                weight_pass(1 - which, part).wait_recv()

    def rs_copy(t, k, slot):
        dst = (rs_n, rs_g)[t]
        return remote(
            rs_send.at[slot, t], dst.at[pl.ds(k * cap, cap)], r_send.at[t, k], r_recv.at[t, k], core_peer
        )

    def back_copy(t, k):
        src, dst = ((rs_n, back_n), (rs_g, back_g))[t]
        e = flip(z, k)
        return remote(
            src.at[pl.ds(k * cap, cap)], dst.at[slots(z)], b_send.at[t, k], b_recv.at[t, k], (dp, e, h)
        )

    def back_local(t):
        src, dst = ((rs_n, back_n), (rs_g, back_g))[t]
        return pltpu.make_async_copy(src.at[pl.ds(0, cap)], dst.at[slots(z)], local.at[t, 0])

    for turn, k in enumerate(order):
        source = flip(z, k)
        slot = turn % 2
        for t in (0, 1):
            if k:
                z_copy(t, k).wait_recv()
                pair_copy(t, k).start()
        for t in (0, 1):
            pair_copy(t, k).wait_recv()
        chunk = pl.ds(pl.multiple_of(source * 2 * cap, 2 * cap), 2 * cap)
        for half, (first, second) in enumerate(((win_ref, wout_ref), (wp_in, wp_out))):
            @pl.loop(0, hid // hidden_tile)
            def _(j):
                cols = pl.ds(pl.multiple_of(j * hidden_tile, hidden_tile), hidden_tile)
                pre = dot_nn(xs[chunk, :], first[:, cols])
                back = dot_nt(gs[chunk, :], second[cols, :])
                square = pre * pre
                curve = jnp.tanh(C0 * pre * (1.0 + C1 * square))
                low_half = 0.5 * (1.0 + curve)
                slope = low_half + (0.5 * C0) * pre * (1.0 - curve * curve) * (1.0 + (3.0 * C1) * square)
                at = pl.ds(pl.multiple_of(half * hid + j * hidden_tile, hidden_tile), hidden_tile)
                hs[chunk, at] = (pre * low_half).astype(BF16)
                ps[chunk, at] = (back * slope).astype(BF16)

        def partial_n(rows):
            return dot_nn(hs[rows, pl.ds(0, hid)], wout_ref[...]) + dot_nn(hs[rows, pl.ds(hid, hid)], wp_out[...])

        def partial_g(rows):
            return dot_nt(ps[rows, pl.ds(0, hid)], win_ref[...]) + dot_nt(ps[rows, pl.ds(hid, hid)], wp_in[...])

        theirs, ours = arrive(source, 1 - c), arrive(source, c)
        if turn >= 2:
            for t in (0, 1):
                rs_copy(t, order[turn - 2], slot).wait_send()
        rs_send[slot, 0] = partial_n(theirs).astype(BF16)
        rs_copy(0, k, slot).start()
        rs_send[slot, 1] = partial_g(theirs).astype(BF16)
        rs_copy(1, k, slot).start()
        own_n[...] = partial_n(ours)
        own_g[...] = partial_g(ours)
        for t, (own, got) in enumerate(((own_n, rs_n), (own_g, rs_g))):
            rs_copy(t, k, slot).wait_recv()
            span = pl.ds(k * cap, cap)
            got[span, :] = (own[...] + got[span, :].astype(F32)).astype(BF16)
            if k:
                back_copy(t, k).start()
            else:
                back_local(t).start()

    for which in (0, 1):
        @pl.when(parity == which)
        def _():
            for part in range(weight_parts):
                weight_copy(which, part).wait_send()
                weight_pass(which, part).wait_send()

    heights = (width // grad_parts, hid // grad_parts)
    piece = 128

    def span_of(t, i, sub=None):
        if sub is None:
            return pl.ds(pl.multiple_of(i * heights[t], heights[t]), heights[t])
        return pl.ds(pl.multiple_of(i * heights[t] + sub * piece, piece), piece)

    pieces = [(t, sub) for t in (0, 1) for sub in range(heights[t] // piece)]

    def y_copy(t, i, sub):
        src, dst = ((wp_in, y_in), (wp_out, y_out))[t]
        span, at = span_of(t, i, sub), i * (heights[t] // piece) + sub
        return remote(src.at[span], dst.at[span], y_send.at[t, at], y_recv.at[t, at], y_peer)

    def d_copy(t, i, sub):
        src, dst = ((y_in, gb_in), (y_out, gb_out))[t]
        span, at = span_of(t, i, sub), i * (heights[t] // piece) + sub
        return remote(src.at[span], dst.at[span], d_send.at[t, at], d_recv.at[t, at], x_peer)

    def d_local(t, i, sub):
        src, dst = ((y_in, ga_in), (y_out, ga_out))[t]
        span, at = span_of(t, i, sub), i * (heights[t] // piece) + sub
        return pltpu.make_async_copy(src.at[span], dst.at[span], local.at[2 + t, at])

    def weight_grad(t, i, half):
        if t == 0:
            return dot_tn(xs[:, span_of(0, i)], ps[:, pl.ds(half * hid, hid)])
        at = pl.ds(pl.multiple_of(half * hid + i * heights[1], heights[1]), heights[1])
        return dot_tn(hs[:, at], gs[...])

    @pl.loop(0, grad_parts)
    def _(i):
        for t in (0, 1):
            (wp_in, wp_out)[t][span_of(t, i), :] = weight_grad(t, i, 1).astype(BF16)
            for sub in range(heights[t] // piece):
                y_copy(t, i, sub).start()

    @pl.loop(0, grad_parts)
    def _(i):
        for t in (0, 1):
            mine = weight_grad(t, i, 0)
            got = (y_in, y_out)[t]
            for sub in range(heights[t] // piece):
                span = span_of(t, i, sub)
                y_copy(t, i, sub).wait_recv()
                got[span, :] = (mine[sub * piece:(sub + 1) * piece] + got[span, :].astype(F32)).astype(BF16)
                if pairs == 2:
                    d_copy(t, i, sub).start()
                d_local(t, i, sub).start()

    for k in range(1, experts):
        for t in (0, 1):
            z_copy(t, k).wait_send()
            back_copy(t, k).wait_recv()
            back_copy(t, k).wait_send()
    for t in (0, 1):
        back_local(t).wait()
        got = pltpu.make_async_copy((back_n, back_g)[t], (bn, bg)[t], local.at[t, 0])
        got.start()
        got.wait()

    total[...] = jnp.zeros_like(total)

    @pl.loop(0, tokens // tile)
    def _(i):
        rows = pl.ds(pl.multiple_of(i * tile, tile), tile)
        spots = place[rows, :]
        expert_out = dot_nn(spots, bn[...])
        expert_g = dot_nn(spots, bg[...])
        x = x_ref[rows, :].astype(F32)
        up = cot_ref[rows, :].astype(F32)
        g, inverse, soft = gate[rows, :], inv[rows, :], probs[rows, :]
        hot = (route_ref[rows, :] == lax.broadcasted_iota(jnp.int32, (tile, experts), 1)).astype(F32)
        act_ref[rows, :] = (x + g * expert_out).astype(BF16)
        gate_g = jnp.sum(up * expert_out, axis=1, keepdims=True)
        logit_g = gate_g * g * (hot - soft)
        low = normed[rows, :].astype(F32)
        total[pl.ds(0, experts), :] += lax.dot_general(
            logit_g, low, (((0,), (0,)), ((), ())), precision=HIGHEST, preferred_element_type=F32
        )
        normed_router = lax.dot_general(
            logit_g, router_ref[...].astype(F32), (((1,), (1,)), ((), ())),
            precision=HIGHEST, preferred_element_type=F32,
        )
        normed_g = expert_g + normed_router
        total[pl.ds(experts, 1), :] += jnp.sum(normed_g * x * inverse, axis=0, keepdims=True)
        u = gain_ref[...].astype(F32) * normed_g
        dot = jnp.sum(u * x, axis=1, keepdims=True)
        ig_ref[rows, :] = up + inverse * u - x * (inverse * inverse * inverse * dot / width)

    steps = [core_peer, y_peer] + [(flip(dp, m), z, h) for m in dp_steps]
    steps += [(dp, flip(z, m), h) for m in [1 << s for s in range(8)] if m < experts]
    for s, peer in enumerate(steps):
        copy = remote(total, red_in.at[s], red_send.at[s], red_recv.at[s], peer)
        copy.start()
        copy.wait()
        total[...] += red_in[s]
    red_ref[...] = total[...]

    for k in range(experts):
        for t in (0, 1):
            pair_copy(t, k).wait_send()
    for turn in range(max(0, experts - 2), experts):
        for t in (0, 1):
            rs_copy(t, order[turn], turn % 2).wait_send()

    @pl.loop(0, grad_parts)
    def _(i):
        for t, sub in pieces:
            y_copy(t, i, sub).wait_send()
            d_local(t, i, sub).wait()
            if pairs == 2:
                d_copy(t, i, sub).wait()


def on_device(tokens, route, norm_gain, router_weight, w_in, w_out, cotangent):
    rows, width = tokens.shape
    experts = lax.axis_size("expert")
    pairs = lax.axis_size("dp")
    cap = 2 * rows // experts
    hid = w_in.shape[2]
    order = [0, 2, 3, 1] + list(range(4, experts))
    order = [k for k in order if k < experts]
    hidden_tile = 256
    weight_parts, grad_parts = 4, 3
    grad_pieces = max(width, hid) // 128
    slot_rows = experts * cap
    both = 2 * slot_rows
    red_rows = 8 * ((experts + 1 + 7) // 8)
    reduce_steps = 2 + (pairs - 1).bit_length() + (experts - 1).bit_length()
    vmem = pl.BlockSpec(memory_space=pltpu.VMEM)
    hbm = pl.BlockSpec(memory_space=pl.ANY)
    sem = pltpu.SemaphoreType.DMA
    shape = jax.ShapeDtypeStruct
    out = pl.pallas_call(
        functools.partial(block_kernel, experts, pairs, order, hidden_tile, weight_parts, grad_parts),
        out_shape=[
            shape((rows, width), BF16),
            shape((rows, width), F32),
            shape((red_rows, width), F32),
            shape((width, hid), BF16),
            shape((hid, width), BF16),
            shape((width, hid), BF16),
            shape((hid, width), BF16),
            shape((slot_rows, width), BF16),
            shape((slot_rows, width), BF16),
        ],
        in_specs=[vmem] * 7,
        out_specs=[vmem] * 3 + [hbm] * 6,
        scratch_shapes=[
            pltpu.VMEM((rows, width), BF16),
            pltpu.VMEM((rows, slot_rows), BF16),
            pltpu.VMEM((rows, 1), F32),
            pltpu.VMEM((rows, 1), F32),
            pltpu.VMEM((rows, experts), F32),
            pltpu.VMEM((slot_rows, width), BF16),
            pltpu.VMEM((slot_rows, width), BF16),
            pltpu.VMEM((both, width), BF16),
            pltpu.VMEM((both, width), BF16),
            pltpu.VMEM((both, 2 * hid), BF16),
            pltpu.VMEM((both, 2 * hid), BF16),
            pltpu.VMEM((width, hid), BF16),
            pltpu.VMEM((hid, width), BF16),
            pltpu.VMEM((width, hid), BF16),
            pltpu.VMEM((hid, width), BF16),
            pltpu.VMEM((2, 2, cap, width), BF16),
            pltpu.VMEM((slot_rows, width), BF16),
            pltpu.VMEM((slot_rows, width), BF16),
            pltpu.VMEM((cap, width), F32),
            pltpu.VMEM((cap, width), F32),
            pltpu.VMEM((red_rows, width), F32),
            pltpu.VMEM((reduce_steps, red_rows, width), F32),
            sem((weight_parts,)), sem((weight_parts,)), sem((weight_parts,)), sem((weight_parts,)),
            sem((2, experts)), sem((2, experts)), sem((2, experts)), sem((2, experts)),
            sem((2, experts)), sem((2, experts)), sem((2, experts)), sem((2, experts)),
            sem((2, grad_pieces)), sem((2, grad_pieces)), sem((2, grad_pieces)), sem((2, grad_pieces)),
            sem((reduce_steps,)), sem((reduce_steps,)), sem((4, grad_pieces)),
        ],
        compiler_params=pltpu.CompilerParams(
            collective_id=0, has_side_effects=True, vmem_limit_bytes=62 * 1024 * 1024
        ),
    )(tokens, route, norm_gain[None, :], router_weight, w_in[0], w_out[0], cotangent)
    activations, input_grad, red, ga_in, ga_out, gb_in, gb_out = out[:7]
    if pairs == 2:
        first_grad = ga_in.astype(F32) + gb_in.astype(F32)
        second_grad = ga_out.astype(F32) + gb_out.astype(F32)
    else:
        first_grad, second_grad = lax.psum((ga_in.astype(F32), ga_out.astype(F32)), "dp")
    return (
        activations, input_grad, red[experts], red[:experts].T, first_grad[None], second_grad[None],
    )


def solution(mesh):
    placed = (
        P(AXES, None),
        P(AXES, None),
        P(),
        P(),
        P("expert", None, "hidden"),
        P("expert", "hidden", None),
        P(AXES, None),
    )
    return jax.shard_map(
        on_device,
        mesh=mesh,
        in_specs=placed,
        out_specs=(
            P(AXES, None),
            P(AXES, None),
            P(),
            P(),
            P("expert", None, "hidden"),
            P("expert", "hidden", None),
        ),
        check_vma=False,
    )
```

time: 1400 us -> 319 us (0.23)
  waiting for transfers between devices: 928 us -> 0 us
  Pallas kernels: 0 us -> 301 us
  starting transfers between devices: 168 us -> 0 us
  blocking collectives: 115 us -> 0 us
  matrix products: 109 us -> 0 us
  other arithmetic: 38.7 us -> 6.47 us
  local copies, waits for them, and re-layouts: 28.2 us -> 10.7 us
    all_to_all x4 -> x0, waiting for transfers between devices: 928 us -> none  [the longest x2 614 us: return_rows(): lax.all_to_all(shaped, ('expert', 'hidden'), split_axis=0, concat_axis=0,...]
    pallas_call x0 -> x1, Pallas kernels: none -> 301 us  [on_device(): pl.pallas_call(functools.partial(block_kernel, experts, pairs, order, hid...]
    all_to_all x4 -> x0, starting transfers between devices: 168 us -> none  [the longest x2 120 us: return_rows(): lax.all_to_all(shaped, ('expert', 'hidden'), split_axis=0, concat_axis=0,...]
    psum x1 -> x0, blocking collectives: 115 us -> none  [on_device(): lax.psum((gain_part, router_part), ('dp', 'expert', 'hidden'))]
    dot_general x9 -> x0, matrix products: 109 us -> none  [the longest x1 23.1 us: on_device(): jnp.dot(pre_grad, first_weight.T, preferred_element_type=jnp.float32)]
    reduce_sum x7 -> x0, other arithmetic: 19.9 us -> none  [the longest x2 15.6 us: return_rows(): jnp.sum(returned.reshape(expert_count, hidden_count, capacity, width), ax...]
  transfers between devices with their start and end apart: 5 -> 0, of which waited for: 4 -> 0; matrix products, arithmetic and copies ran while one was open for 7% -> 0% of each run, Pallas kernels for 0% -> 0%
where the time goes in v1:
time: 319 us
  Pallas kernels  301 us (94%)
  local copies, waits for them, and re-layouts  10.7 us (3%)
  other arithmetic  6.47 us (2%)
    pallas_call x1, Pallas kernels, on_device(): pl.pallas_call(functools.partial(block_kernel, experts, pairs, order, hid...  301 us
    unnamed x12, local copies, waits for them, and re-layouts  6.65 us

profile of v1, /device:TPU:0, one launch (start us, length us, event | category | flops | bytes accessed | tf_op | source)
XLA Modules:
  0.0 318.9 jit_solution(6808474788410305451)
XLA Ops:
  0.6 1.3 broadcast_in_dim.9.gain_ref
  1.9 1.5 copy.13.route_ref
  3.5 1.6 copy.14.router_ref
  5.1 301.1 %shard_map.118 = (bf16[512,1152]{1,0:T(8,128)(2,1)}, f32[512,1152]{1,0:T(8,128)}, f32[8,1152]{1,0:T(8,128)}, bf16[1152,768]{1,0:T(8,128)(2,1)}, bf16[768,1152]{1...) custom-call(bf16[512,1152]{1,0:T(8,128)(2,1)} %x_ref.1, ...), custom_call_target="tpu_custom_call" | custom-call | tf_op jit(solution)/shard_map/pallas_call | solution.py:373
  306.1 1.4 slice_reduce_fusion
  307.5 1.4 slice_bitcast_fusion
  308.9 0.0 copy-start.1
  308.9 0.0 copy-start.2
  308.9 4.3 %add_bitcast_fusion.1 = f32[1,1152,768]{2,1,0:T(8,128)} fusion(bf16[1152,768]{1,0:T(8,128)(2,1)} %get-tuple-element.17, bf16[1152,768]{1,0:T(8,128)(2,1)} %get-tuple-element.16), kind=kLoop, calls=%fused_computation.1 | loop fusion | flops 2654208 | bytes 7077888 | tf_op jit(solution)/shard_map/broadcast_in_dim | solution.py:428
  313.2 0.0 copy-done.1
  313.2 0.0 copy-done.2
  313.2 0.0 copy-start.3
  313.2 2.1 add_bitcast_fusion
  315.4 0.0 copy-done.3
  315.4 0.0 copy-start
  315.4 1.0 copy.17
  316.4 1.1 copy-done
  317.5 1.4 copy.18
Async XLA Ops:
  308.9 4.3 %copy-start.1 = (bf16[768,1152]{1,0:T(8,128)(2,1)S(1)}, bf16[768,1152]{1,0:T(8,128)(2,1)}, u32[]{:S(2)}) copy-start(bf16[768,1152]{1,0:T(8,128)(2,1)} %get-tuple-element.18) | copy-start | bytes 5308420
  308.9 4.3 %copy-start.2 = (bf16[768,1152]{1,0:T(8,128)(2,1)S(1)}, bf16[768,1152]{1,0:T(8,128)(2,1)}, u32[]{:S(2)}) copy-start(bf16[768,1152]{1,0:T(8,128)(2,1)} %get-tuple-element.19) | copy-start | bytes 5308420
  313.2 2.1 copy-start.3
  315.4 2.1 copy-start

commit v2 on v0

v2 whole, which is shorter than its diff:
```python
import functools

import jax
import jax.numpy as jnp
from jax import lax
from jax.experimental import pallas as pl
from jax.experimental.pallas import tpu as pltpu
from jax.sharding import PartitionSpec as P

HIGHEST = lax.Precision.HIGHEST
MESH = pl.DeviceIdType.MESH
EPSILON = 1e-05
F32 = jnp.float32
BF16 = jnp.bfloat16
AXES = ("dp", "expert", "hidden")
C0 = 0.7978845608
C1 = 0.044715
TILE = 128
PIECE = 128
SMALL = 64


def flip(index, mask, limit):
    out, bit = 0, 1
    while bit < limit:
        a, b = lax.rem(lax.div(index, bit), 2), lax.rem(lax.div(mask, bit), 2)
        out = out + bit * (a + b - 2 * a * b)
        bit *= 2
    return out


def contract(a, b, left, right, **kwargs):
    return lax.dot_general(a, b, (((left,), (right,)), ((), ())), preferred_element_type=F32, **kwargs)


def dot_nn(a, b):
    return contract(a, b, 1, 0)


def dot_nt(a, b):
    return contract(a, b, 1, 1)


def dot_tn(a, b):
    return contract(a, b, 0, 0)


def remote(src, dst, send, recv, peer):
    return pltpu.make_async_remote_copy(
        src_ref=src, dst_ref=dst, send_sem=send, recv_sem=recv, device_id=peer, device_id_type=MESH
    )


def plane_peer(i, pairs, halves):
    dp, z, h = (lax.axis_index(a) for a in AXES)
    return lax.rem(dp + lax.div(i, halves), pairs), z, lax.rem(h + lax.rem(i, halves), halves)


def line_peer(i, experts):
    dp, z, h = (lax.axis_index(a) for a in AXES)
    return dp, lax.rem(z + i, experts), h


def signal_all(pairs, experts, halves):
    barrier = pltpu.get_barrier_semaphore()

    @pl.loop(1, pairs * halves)
    def _(i):
        pl.semaphore_signal(barrier, inc=1, device_id=plane_peer(i, pairs, halves), device_id_type=MESH)

    @pl.loop(1, experts)
    def _(i):
        pl.semaphore_signal(barrier, inc=1, device_id=line_peer(i, experts), device_id_type=MESH)


def wait_all(pairs, experts, halves):
    pl.semaphore_wait(pltpu.get_barrier_semaphore(), pairs * halves + experts - 2)


def prologue_kernel(
    experts, pairs, halves, cold,
    x_hbm, route_ref, gain_ref, router_ref, cot_hbm,
    bn_out, bg_out, aux_ref, level_ref,
    x_ref, cot_ref, place, router, ranks, stage, counts, count_in, line_in, send, recv, load, local,
):
    tokens, width = x_ref.shape
    cap = bn_out.shape[0] // experts
    signal_all(pairs, experts, halves)
    loads = [
        pltpu.make_async_copy(src, dst, load.at[i])
        for i, (src, dst) in enumerate(((x_hbm, x_ref), (cot_hbm, cot_ref)))
    ]
    for copy in loads:
        copy.start()

    lane = lax.broadcasted_iota(jnp.int32, (tokens, TILE), 1)
    chosen = jnp.transpose(jnp.broadcast_to(route_ref[...].astype(F32), (TILE, tokens)))
    onehot = (chosen.astype(jnp.int32) == lane).astype(F32)
    counts[...] = jnp.broadcast_to(jnp.sum(onehot, axis=0, keepdims=True), (8, TILE))
    before = (
        lax.broadcasted_iota(jnp.int32, (tokens, tokens), 1) < lax.broadcasted_iota(jnp.int32, (tokens, tokens), 0)
    ).astype(BF16)
    rank = jnp.sum(dot_nn(before, onehot.astype(BF16)) * onehot, axis=1, keepdims=True)
    ranks[0] = chosen
    ranks[1] = chosen * cap + rank
    router[...] = jnp.zeros_like(router)
    router[pl.ds(0, experts), :] = router_ref[...]

    here = pairs * halves

    def plane_copy(i):
        return remote(counts, count_in.at[i], send.at[i], recv.at[i], plane_peer(i, pairs, halves))

    def line_copy(i):
        at = here - 1 + i
        return remote(count_in.at[0], line_in.at[i], send.at[at], recv.at[at], line_peer(i, experts))

    wait_all(pairs, experts, halves)

    @pl.loop(1, here)
    def _(i):
        plane_copy(i).start()

    for copy in loads:
        copy.wait()

    @pl.loop(0, tokens // TILE)
    def _(i):
        rows = pl.ds(pl.multiple_of(i * TILE, TILE), TILE)
        x = x_ref[rows, :].astype(F32)
        inverse = lax.rsqrt(jnp.mean(x * x, axis=1, keepdims=True) + EPSILON)
        low = (x * inverse * gain_ref[...].astype(F32)).astype(BF16)
        x_ref[rows, :] = low
        lanes = lax.broadcasted_iota(jnp.int32, (TILE, TILE), 1)
        expert, slot = ranks[0, rows, :], ranks[1, rows, :]
        logits = jnp.where(lanes < experts, dot_nt(low, router[...]), -jnp.inf)
        shifted = jnp.exp(logits - jnp.max(logits, axis=1, keepdims=True))
        soft = shifted / jnp.sum(shifted, axis=1, keepdims=True)
        gate = jnp.sum(jnp.where(expert.astype(jnp.int32) == lanes, soft, 0.0), axis=1, keepdims=True)
        cot_ref[rows, :] = (gate * cot_ref[rows, :].astype(F32)).astype(BF16)
        aux = jnp.where(lanes == experts, gate, soft)
        aux = jnp.where(lanes == experts + 1, inverse, aux)
        aux = jnp.where(lanes == experts + 2, slot, aux)
        aux_ref[rows, :] = jnp.where(lanes == experts + 3, expert, aux)
        slot_int = slot.astype(jnp.int32)
        for j in range(experts * cap // TILE):
            place[rows, pl.ds(j * TILE, TILE)] = (slot_int == lanes + j * TILE).astype(BF16)

    most = counts[...]
    for i in range(1, here):
        plane_copy(i).wait_recv()
        most = jnp.maximum(most, count_in[i])
    count_in[0] = most

    @pl.loop(1, experts)
    def _(i):
        line_copy(i).start()

    def out_copy(t, e):
        span = pl.ds(pl.multiple_of(e * cap, cap), cap)
        return pltpu.make_async_copy(stage.at[t, span], (bn_out, bg_out)[t].at[span], local.at[t, e])

    @pl.loop(0, experts)
    def _(e):
        span = pl.ds(pl.multiple_of(e * cap, cap), cap)
        for t, values in enumerate((x_ref, cot_ref)):
            stage[t, span, :] = dot_tn(place[:, span], values[...]).astype(BF16)
            out_copy(t, e).start()

    most = count_in[0]
    for i in range(1, experts):
        line_copy(i).wait_recv()
        most = jnp.maximum(most, line_in[i])
    lanes = lax.broadcasted_iota(jnp.int32, (8, TILE), 1)
    rows = lax.broadcasted_iota(jnp.int32, (8, TILE), 0)
    over = jnp.where((most > cold) & (rows == 0), 1.0, 0.0)
    crowded = jnp.sum(over)
    which = jnp.sum(over * lanes.astype(F32))
    level_ref[0] = jnp.where(crowded <= 1.0, which, float(experts)).astype(jnp.int32)

    @pl.loop(1, here)
    def _(i):
        plane_copy(i).wait_send()

    @pl.loop(1, experts)
    def _(i):
        line_copy(i).wait_send()

    @pl.loop(0, experts)
    def _(e):
        for t in (0, 1):
            out_copy(t, e).wait()


def block_kernel(
    experts, pairs, halves, hot, cold, hidden_tile, weight_parts, grad_parts,
    x_hbm, aux_hbm, gain_ref, router_ref, win_hbm, wout_hbm, cot_hbm, bn, bg,
    act_hbm, ig_hbm, red_ref, ga_in, ga_out, gb_in, gb_out,
    x_ref, cot_ref, aux_ref, w_in, w_out, act_ref, ig_ref,
    xs, gs, hs, ps, g_in, g_out, y_in, y_out,
    rs_send, rs_n, rs_g, acc_n, acc_g, acc_in, logits, ret_n, ret_g, total, red_plane, red_line,
    w_send, w_recv, wf_send, wf_recv, z_send, z_recv, f_send, f_recv, r_send, r_recv,
    b_send, b_recv, y_send, y_recv, d_send, d_recv, red_send, red_recv, load, local, out_sem, all_in,
):
    tokens, width = x_ref.shape
    hid = w_in.shape[2]
    cap = bn.shape[0] // experts
    dp, z, h = (lax.axis_index(a) for a in AXES)
    c = lax.rem(h, 2)
    parity = lax.rem(dp, 2)
    core_peer = (dp, z, flip(h, 1, halves))
    y_peer = (dp, z, flip(h, 2, halves))
    x_peer = (flip(dp, 1, pairs), z, h)
    here = pairs * halves
    signal_all(pairs, experts, halves)
    wait_all(pairs, experts, halves)

    def sized(e, act):
        if hot is None:
            act(cap)
        else:
            @pl.when(e == hot)
            def _():
                act(cap)

            @pl.when(e != hot)
            def _():
                act(cold)

    def slots(e, rows=cap):
        return pl.ds(pl.multiple_of(e * cap, cap), rows)

    def arrive(source, core, rows=cap):
        return pl.ds(pl.multiple_of((source * 2 + core) * cap, cap), rows)

    def turn_k(turn):
        return flip(turn, lax.div(turn, 2), experts)

    def z_copy(t, k, rows):
        src, dst = ((bn, xs), (bg, gs))[t]
        e = flip(z, k, experts)
        return remote(
            src.at[slots(e, rows)], dst.at[arrive(z, c, rows)], z_send.at[t, k], z_recv.at[t, k], (dp, e, h)
        )

    def z_start(t, k):
        sized(flip(z, k, experts), lambda rows: z_copy(t, k, rows).start())

    early = max(1, experts - 1)

    @pl.loop(1, early)
    def _(n):
        for t in (0, 1):
            z_start(t, turn_k(early - n))

    mats = ((win_hbm, w_in), (wout_hbm, w_out))

    def weight_copy(which, part):
        src, dst = mats[which]
        rows = src.shape[0] // weight_parts
        span = pl.ds(pl.multiple_of(part * rows, rows), rows)
        return remote(src.at[span], dst.at[1, span], w_send.at[part], w_recv.at[part], y_peer)

    def weight_pass(which, part):
        dst = mats[which][1]
        rows = dst.shape[1] // weight_parts
        span = pl.ds(pl.multiple_of(part * rows, rows), rows)
        return remote(dst.at[1, span], dst.at[1, span], wf_send.at[part], wf_recv.at[part], x_peer)

    for which in (0, 1):
        @pl.when(parity == which)
        def _():
            @pl.loop(0, weight_parts)
            def _(part):
                weight_copy(which, part).start()

    def pair_copy(t, k, rows):
        buf = (xs, gs)[t]
        span = arrive(flip(z, k, experts), c, rows)
        return remote(buf.at[span], buf.at[span], f_send.at[t, k], f_recv.at[t, k], core_peer)

    def own_pair(t, rows):
        src, dst = ((bn, xs), (bg, gs))[t]
        return remote(
            src.at[slots(z, rows)], dst.at[arrive(z, c, rows)], f_send.at[t, 0], f_recv.at[t, 0], core_peer
        )

    def own_local(t, rows):
        src, dst = ((bn, xs), (bg, gs))[t]
        return pltpu.make_async_copy(src.at[slots(z, rows)], dst.at[arrive(z, c, rows)], load.at[t])

    for t in (0, 1):
        sized(z, lambda rows: own_pair(t, rows).start())
        sized(z, lambda rows: own_local(t, rows).start())
    loads = [
        pltpu.make_async_copy(src, dst, load.at[2 + i])
        for i, (src, dst) in enumerate(
            (
                (win_hbm, w_in.at[0]), (wout_hbm, w_out.at[0]),
                (x_hbm, x_ref), (cot_hbm, cot_ref), (aux_hbm, aux_ref),
            )
        )
    ]
    for copy in loads:
        copy.start()

    if hot is not None:
        @pl.when(z != hot)
        def _():
            @pl.loop(0, 2 * experts)
            def _(i):
                rest = pl.ds(pl.multiple_of(i * cap, cap) + cold, cap - cold)
                xs[rest, :] = jnp.zeros((cap - cold, width), BF16)
                gs[rest, :] = jnp.zeros((cap - cold, width), BF16)

        @pl.loop(0, experts)
        def _(e):
            @pl.when(e != hot)
            def _():
                rest = pl.ds(pl.multiple_of(e * cap, cap) + cold, cap - cold)
                ret_n[rest, :] = jnp.zeros((cap - cold, width), BF16)
                ret_g[rest, :] = jnp.zeros((cap - cold, width), BF16)

    for copy in loads:
        copy.wait()
    for t in (0, 1):
        sized(z, lambda rows: own_local(t, rows).wait())

    for which in (0, 1):
        @pl.when(parity == which)
        def _():
            @pl.loop(0, weight_parts)
            def _(part):
                weight_copy(which, part).wait_recv()
                weight_pass(which, part).start()

    final = turn_k(experts - 1)
    if experts > 1:
        for t in (0, 1):
            if experts > 2:
                k = turn_k(experts - 2)
                sized(flip(z, k, experts), lambda rows: z_copy(t, k, rows).wait_send())
            z_start(t, final)

    for which in (0, 1):
        @pl.when(parity == which)
        def _():
            @pl.loop(0, weight_parts)
            def _(part):
                weight_pass(1 - which, part).wait_recv()
                weight_copy(which, part).wait_send()
                weight_pass(which, part).wait_send()

    def token_block(turn):
        k = turn_k(turn)
        source = flip(z, k, experts)

        @pl.when(turn > 0)
        def _():
            for t in (0, 1):
                sized(z, lambda rows: z_copy(t, k, rows).wait_recv())
                sized(z, lambda rows: pair_copy(t, k, rows).start())

        @pl.when(turn == experts - 1)
        def _():
            @pl.loop(1, experts)
            def _(i):
                pl.semaphore_signal(all_in, inc=1, device_id=line_peer(i, experts), device_id_type=MESH)

        for t in (0, 1):
            sized(z, lambda rows: pair_copy(t, k, rows).wait_recv())
        chunk = pl.ds(pl.multiple_of(source * 2 * cap, 2 * cap), 2 * cap)
        per_half = hid // hidden_tile

        @pl.loop(0, 2 * per_half)
        def _(j):
            half = lax.div(j, per_half)
            cols = pl.ds(pl.multiple_of(lax.rem(j, per_half) * hidden_tile, hidden_tile), hidden_tile)
            pre = dot_nn(xs[chunk, :], w_in[half, :, cols])
            back = dot_nt(gs[chunk, :], w_out[half, cols, :])
            square = pre * pre
            curve = jnp.tanh(C0 * pre * (1.0 + C1 * square))
            low_half = 0.5 * (1.0 + curve)
            slope = low_half + (0.5 * C0) * pre * (1.0 - curve * curve) * (1.0 + (3.0 * C1) * square)
            at = pl.ds(pl.multiple_of(j * hidden_tile, hidden_tile), hidden_tile)
            hs[chunk, at] = (pre * low_half).astype(BF16)
            ps[chunk, at] = (back * slope).astype(BF16)

            @pl.when((turn == experts - 1) & (j == 1))
            def _():
                pl.semaphore_wait(all_in, experts - 1)

                @pl.loop(1, experts - 1)
                def _(earlier):
                    held(earlier)

    def rs_copy(t, k, slot):
        return remote(
            rs_send.at[slot, t], (rs_n, rs_g)[t].at[slots(k)], r_send.at[t, k], r_recv.at[t, k], core_peer
        )

    def back_copy(t, k, rows):
        src, dst = ((rs_n, ret_n), (rs_g, ret_g))[t]
        return remote(
            src.at[slots(k, rows)], dst.at[slots(z, rows)], b_send.at[t, k], b_recv.at[t, k],
            (dp, flip(z, k, experts), h),
        )

    def back_start(turn):
        k = turn_k(turn)
        for t in (0, 1):
            sized(z, lambda rows: back_copy(t, k, rows).start())

    def held(turn):
        if hot is None:
            back_start(turn)
        else:
            @pl.when(z != hot)
            def _():
                back_start(turn)

    def token_sums(turn):
        k = turn_k(turn)
        source = flip(z, k, experts)
        slot = lax.rem(turn, 2)

        @pl.when(turn >= 2)
        def _():
            for t in (0, 1):
                rs_copy(t, turn_k(turn - 2), slot).wait_send()

        @pl.loop(0, 2)
        def _(mine):
            rows = arrive(source, lax.rem(1 + c + mine, 2))
            for t, (values, weights, dot, acc) in enumerate(
                ((hs, w_out, dot_nn, acc_n), (ps, w_in, dot_nt, acc_g))
            ):
                acc = acc.at[pl.ds(0, cap)]
                acc[...] = dot(values[rows, pl.ds(0, hid)], weights[0])
                acc[...] += dot(values[rows, pl.ds(hid, hid)], weights[1])

                @pl.when(mine == 0)
                def _():
                    rs_send[slot, t] = acc[...].astype(BF16)
                    rs_copy(t, k, slot).start()

        for t, (acc, got, home) in enumerate(((acc_n, rs_n, ret_n), (acc_g, rs_g, ret_g))):
            rs_copy(t, k, slot).wait_recv()
            both = (acc[pl.ds(0, cap), :] + got[slots(k), :].astype(F32)).astype(BF16)

            @pl.when(turn == 0)
            def _():
                home[slots(z), :] = both

            @pl.when(turn > 0)
            def _():
                got[slots(k), :] = both

    heights = (width // grad_parts, hid // grad_parts)
    subs = tuple(height // PIECE for height in heights)

    def grad_span(t, i, sub=None):
        if sub is None:
            return pl.ds(pl.multiple_of(i * heights[t], heights[t]), heights[t])
        return pl.ds(pl.multiple_of(i * heights[t] + sub * PIECE, PIECE), PIECE)

    def y_copy(t, i, sub):
        src, dst = ((g_in, y_in), (g_out, y_out))[t]
        span, at = grad_span(t, i, sub), i * subs[t] + sub
        return remote(src.at[span], dst.at[span], y_send.at[t, at], y_recv.at[t, at], y_peer)

    def d_copy(t, i, sub):
        src, dst = ((y_in, gb_in), (y_out, gb_out))[t]
        span, at = grad_span(t, i, sub), i * subs[t] + sub
        return remote(src.at[span], dst.at[span], d_send.at[t, at], d_recv.at[t, at], x_peer)

    def d_local(t, i, sub):
        src, dst = ((y_in, ga_in), (y_out, ga_out))[t]
        span, at = grad_span(t, i, sub), i * subs[t] + sub
        return pltpu.make_async_copy(src.at[span], dst.at[span], local.at[t, at])

    accs = (acc_in, acc_n)

    def weight_grad(t, i, half):
        accs[t][...] = jnp.zeros_like(accs[t])
        depth = 2 * cap
        at = pl.ds(pl.multiple_of(half * hid, hid), hid)
        if t:
            at = pl.ds(pl.multiple_of(half * hid + i * heights[1], heights[1]), heights[1])

        @pl.loop(0, experts)
        def _(n):
            rows = pl.ds(pl.multiple_of(n * depth, depth), depth)
            if t == 0:
                accs[t][...] += dot_tn(xs[rows, grad_span(0, i)], ps[rows, at])
            else:
                accs[t][...] += dot_tn(hs[rows, at], gs[rows, :])

    place = hs.at[pl.ds(0, tokens), pl.ds(0, experts * cap)]
    got_n = ps.at[pl.ds(0, tokens), pl.ds(0, width)]
    got_g = ps.at[pl.ds(tokens, tokens), pl.ds(0, width)]
    normed = hs.at[pl.ds(tokens, tokens), pl.ds(0, width)]

    def unbucket():
        @pl.loop(0, tokens // TILE)
        def _(i):
            rows = pl.ds(pl.multiple_of(i * TILE, TILE), TILE)
            slot = aux_ref[rows, experts + 2:experts + 3].astype(jnp.int32)
            lanes = lax.broadcasted_iota(jnp.int32, (TILE, experts * cap), 1)
            place[rows, :] = (slot == lanes).astype(BF16)

        @pl.loop(0, 3)
        def _(n):
            cols = pl.ds(pl.multiple_of(n * (width // 3), width // 3), width // 3)
            got_n[:, cols] = dot_nn(place[...], ret_n[:, cols]).astype(BF16)
            got_g[:, cols] = dot_nn(place[...], ret_g[:, cols]).astype(BF16)

    def out_copy(t, i):
        rows = pl.ds(pl.multiple_of(i * SMALL, SMALL), SMALL)
        src, dst = ((act_ref, act_hbm), (ig_ref, ig_hbm))[t]
        return pltpu.make_async_copy(src.at[rows], dst.at[rows], out_sem.at[t, i])

    def tokens_tile(i):
        rows = pl.ds(pl.multiple_of(i * SMALL, SMALL), SMALL)
        aux = aux_ref[rows, :]
        soft, g, inverse = aux[:, :experts], aux[:, experts:experts + 1], aux[:, experts + 1:experts + 2]
        chosen = aux[:, experts + 3:experts + 4].astype(jnp.int32)
        expert_out = got_n[rows, :].astype(F32)
        expert_g = got_g[rows, :].astype(F32)
        x = x_ref[rows, :].astype(F32)
        up = cot_ref[rows, :].astype(F32)
        gain = gain_ref[...].astype(F32)
        hits = (chosen == lax.broadcasted_iota(jnp.int32, (SMALL, experts), 1)).astype(F32)
        act_ref[rows, :] = (x + g * expert_out).astype(BF16)
        out_copy(0, i).start()
        gate_g = jnp.sum(up * expert_out, axis=1, keepdims=True)
        logit_g = gate_g * g * (hits - soft)
        logits[rows, :] = logit_g
        normed[rows, :] = (x * inverse * gain).astype(BF16)
        normed_g = expert_g
        for e in range(experts):
            normed_g = normed_g + logit_g[:, e:e + 1] * router_ref[e:e + 1, :].astype(F32)
        total[pl.ds(experts, 1), :] += jnp.sum(normed_g * x * inverse, axis=0, keepdims=True)
        u = gain * normed_g
        dot = jnp.sum(u * x, axis=1, keepdims=True)
        ig_ref[rows, :] = up + inverse * u - x * (inverse * inverse * inverse * dot / width)
        out_copy(1, i).start()

    def router_sum():
        rest = logits[...]
        added = jnp.zeros((experts, width), F32)
        for _ in range(3):
            term = rest.astype(BF16)
            added = added + dot_tn(term, normed[...])
            rest = rest - term.astype(F32)
        total[pl.ds(0, experts), :] = added

    def returned():
        @pl.loop(1, experts)
        def _(turn):
            k = turn_k(turn)
            for t in (0, 1):
                sized(flip(z, k, experts), lambda rows: back_copy(t, k, rows).wait_recv())

    def red_plane_copy(i):
        peer = plane_peer(i, pairs, halves)
        return remote(total, red_plane.at[dp * halves + h], red_send.at[i], red_recv.at[i], peer)

    def red_line_copy(i):
        at = here - 1 + i
        return remote(total, red_line.at[z], red_send.at[at], red_recv.at[at], line_peer(i, experts))

    def token_results():
        returned()
        unbucket()
        total[...] = jnp.zeros_like(total)

        @pl.loop(0, tokens // SMALL)
        def _(i):
            tokens_tile(i)

        router_sum()
        red_plane[dp * halves + h] = total[...]

        @pl.loop(1, here)
        def _(i):
            red_plane_copy(i).start()

    def plane_sum():
        @pl.loop(1, here)
        def _(i):
            red_plane_copy(i).wait()

        added = red_plane[0]
        for i in range(1, here):
            added = added + red_plane[i]
        total[...] = added
        red_line[z] = added

        @pl.loop(1, experts)
        def _(i):
            red_line_copy(i).start()

    def grad_step(step):
        half = jnp.where(step < grad_parts, 1, 0)
        i = lax.rem(step, grad_parts)
        for t in (0, 1):
            weight_grad(t, i, half)
            out, got = ((g_in, y_in), (g_out, y_out))[t]

            @pl.when(half == 1)
            def _():
                out[grad_span(t, i), :] = accs[t][...].astype(BF16)

                @pl.loop(0, subs[t])
                def _(sub):
                    y_copy(t, i, sub).start()

            if t:
                @pl.when(step == 2 * grad_parts - 1)
                def _():
                    token_results()

            @pl.when(half == 0)
            def _():
                @pl.loop(0, subs[t])
                def _(sub):
                    span = grad_span(t, i, sub)
                    y_copy(t, i, sub).wait_recv()
                    mine = accs[t][pl.ds(pl.multiple_of(sub * PIECE, PIECE), PIECE), :]
                    got[span, :] = (mine + got[span, :].astype(F32)).astype(BF16)
                    if pairs == 2:
                        d_copy(t, i, sub).start()
                    d_local(t, i, sub).start()

    @pl.loop(0, experts + 2 * grad_parts)
    def _(step):
        late = experts + 1

        @pl.when(((step > 0) & (step < experts)) | (step == late))
        def _():
            token_sums(jnp.where(step < experts, step, experts) - 1)

        @pl.when(step == late)
        def _():
            back_start(experts - 1)

        if hot is not None:
            @pl.when((step > 1) & (step < experts) & (z == hot))
            def _():
                back_start(step - 1)

        @pl.when(step < experts)
        def _():
            token_block(step)

        @pl.when(step >= experts)
        def _():
            grad_step(step - experts)

    plane_sum()

    @pl.loop(1, experts)
    def _(i):
        red_line_copy(i).wait()

    added = red_line[0]
    for i in range(1, experts):
        added = added + red_line[i]
    red_ref[...] = added

    @pl.loop(1, experts)
    def _(turn):
        k = turn_k(turn)
        for t in (0, 1):
            if experts > 2:
                @pl.when(turn != experts - 2)
                def _():
                    sized(flip(z, k, experts), lambda rows: z_copy(t, k, rows).wait_send())
            else:
                sized(flip(z, k, experts), lambda rows: z_copy(t, k, rows).wait_send())
            sized(z, lambda rows: pair_copy(t, k, rows).wait_send())
            sized(z, lambda rows: back_copy(t, k, rows).wait_send())
    for t in (0, 1):
        sized(z, lambda rows: own_pair(t, rows).wait_send())
        for turn in range(max(0, experts - 2), experts):
            rs_copy(t, turn_k(turn), turn % 2).wait_send()

    @pl.loop(0, tokens // SMALL)
    def _(i):
        for t in (0, 1):
            out_copy(t, i).wait()

    @pl.loop(0, grad_parts)
    def _(i):
        for t in (0, 1):
            @pl.loop(0, subs[t])
            def _(sub):
                y_copy(t, i, sub).wait_send()
                d_local(t, i, sub).wait()
                if pairs == 2:
                    d_copy(t, i, sub).wait()


def finish_kernel(experts, act, ig, red, ai, ao, bi, bo, act_out, ig_out, gain_out, router_out, first_out, second_out):
    act_out[...] = act[...]
    ig_out[...] = ig[...]
    first_out[...] = ai[...].astype(F32) + bi[...].astype(F32)
    second_out[...] = ao[...].astype(F32) + bo[...].astype(F32)

    @pl.when(pl.program_id(0) == 0)
    def _():
        gain_out[...] = red[pl.ds(experts, 1), :]
        router_out[...] = red[pl.ds(0, experts), :]


def on_device(tokens, route, norm_gain, router_weight, w_in, w_out, cotangent):
    rows, width = tokens.shape
    experts = lax.axis_size("expert")
    pairs = lax.axis_size("dp")
    halves = lax.axis_size("hidden")
    cap = 2 * rows // experts
    hid = w_in.shape[2]
    cold = 16 * (-(-11 * cap // 256))
    hidden_tile = 256
    weight_parts, grad_parts = 4, 3
    grad_pieces = max(width, hid) // PIECE
    slot_rows = experts * cap
    both = 2 * slot_rows
    red_rows = 8 * ((experts + 1 + 7) // 8)
    peers = pairs * halves + experts
    vmem = pl.BlockSpec(memory_space=pltpu.VMEM)
    hbm = pl.BlockSpec(memory_space=pl.ANY)
    sem = pltpu.SemaphoreType.DMA
    shape = jax.ShapeDtypeStruct
    params = functools.partial(pltpu.CompilerParams, has_side_effects=True, vmem_limit_bytes=62 * 1024 * 1024)
    gain_row = norm_gain[None, :]
    router_rows = router_weight.T

    bn, bg, aux, level = pl.pallas_call(
        functools.partial(prologue_kernel, experts, pairs, halves, cold),
        out_shape=[
            shape((slot_rows, width), BF16),
            shape((slot_rows, width), BF16),
            shape((rows, TILE), F32),
            shape((1,), jnp.int32),
        ],
        in_specs=[hbm, vmem, vmem, vmem, hbm],
        out_specs=[hbm, hbm, vmem, pl.BlockSpec(memory_space=pltpu.SMEM)],
        scratch_shapes=[
            pltpu.VMEM((rows, width), BF16),
            pltpu.VMEM((rows, width), BF16),
            pltpu.VMEM((rows, slot_rows), BF16),
            pltpu.VMEM((TILE, width), BF16),
            pltpu.VMEM((2, rows, TILE), F32),
            pltpu.VMEM((2, slot_rows, width), BF16),
            pltpu.VMEM((8, TILE), F32),
            pltpu.VMEM((pairs * halves, 8, TILE), F32),
            pltpu.VMEM((experts, 8, TILE), F32),
            sem((peers,)), sem((peers,)), sem((2,)), sem((2, experts)),
        ],
        compiler_params=params(collective_id=0),
    )(tokens, route.T, gain_row, router_rows, cotangent)

    def block(hot):
        return pl.pallas_call(
            functools.partial(
                block_kernel, experts, pairs, halves, hot, cold, hidden_tile, weight_parts, grad_parts
            ),
            out_shape=[
                shape((rows, width), BF16),
                shape((rows, width), F32),
                shape((red_rows, width), F32),
                shape((width, hid), BF16),
                shape((hid, width), BF16),
                shape((width, hid), BF16),
                shape((hid, width), BF16),
            ],
            in_specs=[hbm, hbm, vmem, vmem, hbm, hbm, hbm, hbm, hbm],
            out_specs=[hbm, hbm, vmem, hbm, hbm, hbm, hbm],
            scratch_shapes=[
                pltpu.VMEM((rows, width), BF16),
                pltpu.VMEM((rows, width), BF16),
                pltpu.VMEM((rows, TILE), F32),
                pltpu.VMEM((2, width, hid), BF16),
                pltpu.VMEM((2, hid, width), BF16),
                pltpu.VMEM((rows, width), BF16),
                pltpu.VMEM((rows, width), F32),
                pltpu.VMEM((both, width), BF16),
                pltpu.VMEM((both, width), BF16),
                pltpu.VMEM((both, 2 * hid), BF16),
                pltpu.VMEM((both, 2 * hid), BF16),
                pltpu.VMEM((width, hid), BF16),
                pltpu.VMEM((hid, width), BF16),
                pltpu.VMEM((width, hid), BF16),
                pltpu.VMEM((hid, width), BF16),
                pltpu.VMEM((2, 2, cap, width), BF16),
                pltpu.VMEM((slot_rows, width), BF16),
                pltpu.VMEM((slot_rows, width), BF16),
                pltpu.VMEM((hid // grad_parts, width), F32),
                pltpu.VMEM((cap, width), F32),
                pltpu.VMEM((width // grad_parts, hid), F32),
                pltpu.VMEM((rows, experts), F32),
                pltpu.VMEM((slot_rows, width), BF16),
                pltpu.VMEM((slot_rows, width), BF16),
                pltpu.VMEM((red_rows, width), F32),
                pltpu.VMEM((pairs * halves, red_rows, width), F32),
                pltpu.VMEM((experts, red_rows, width), F32),
                sem((weight_parts,)), sem((weight_parts,)), sem((weight_parts,)), sem((weight_parts,)),
                sem((2, experts)), sem((2, experts)), sem((2, experts)), sem((2, experts)),
                sem((2, experts)), sem((2, experts)), sem((2, experts)), sem((2, experts)),
                sem((2, grad_pieces)), sem((2, grad_pieces)), sem((2, grad_pieces)), sem((2, grad_pieces)),
                sem((peers,)), sem((peers,)), sem((7,)), sem((2, grad_pieces)), sem((2, rows // SMALL)),
                pltpu.SemaphoreType.REGULAR,
            ],
            compiler_params=params(collective_id=1 + (experts if hot is None else hot)),
        )

    operands = (tokens, aux, gain_row, router_rows, w_in[0], w_out[0], cotangent, bn, bg)
    if experts <= 4:
        branches = [block(e) for e in range(experts)] + [block(None)]
        out = lax.switch(level[0], branches, *operands)
    else:
        out = block(None)(*operands)
    act, ig, red, ga_in, ga_out, gb_in, gb_out = out
    if pairs > 2:
        first, second = lax.psum((ga_in.astype(F32), ga_out.astype(F32)), "dp")
        return act, ig, red[experts], red[:experts].T, first[None], second[None]

    steps = 8

    def blocked(array):
        return pl.BlockSpec((array.shape[0] // steps, array.shape[1]), lambda i: (i, 0))

    def whole(array):
        return pl.BlockSpec(array.shape, lambda i: (0, 0))

    outs = [
        shape((rows, width), BF16),
        shape((rows, width), F32),
        shape((1, width), F32),
        shape((experts, width), F32),
        shape((width, hid), F32),
        shape((hid, width), F32),
    ]
    act, ig, gain_grad, router_grad, first, second = pl.pallas_call(
        functools.partial(finish_kernel, experts),
        grid=(steps,),
        out_shape=outs,
        in_specs=[blocked(act), blocked(ig), whole(red)] + [blocked(a) for a in (ga_in, ga_out, gb_in, gb_out)],
        out_specs=[blocked(outs[0]), blocked(outs[1]), whole(outs[2]), whole(outs[3]), blocked(outs[4]), blocked(outs[5])],
    )(act, ig, red, ga_in, ga_out, gb_in, gb_out)
    return act, ig, gain_grad[0], router_grad.T, first[None], second[None]


def solution(mesh):
    placed = (
        P(AXES, None),
        P(AXES, None),
        P(),
        P(),
        P("expert", None, "hidden"),
        P("expert", "hidden", None),
        P(AXES, None),
    )
    return jax.shard_map(
        on_device,
        mesh=mesh,
        in_specs=placed,
        out_specs=(
            P(AXES, None),
            P(AXES, None),
            P(),
            P(),
            P("expert", None, "hidden"),
            P("expert", "hidden", None),
        ),
        check_vma=False,
    )
```

time: 1400 us -> 255 us (0.18)
  waiting for transfers between devices: 928 us -> 0 us
  Pallas kernels: 0 us -> 248 us
  starting transfers between devices: 168 us -> 0 us
  blocking collectives: 115 us -> 0 us
  matrix products: 109 us -> 0 us
  other arithmetic: 38.7 us -> 1.31 us
  local copies, waits for them, and re-layouts: 28.2 us -> 1.42 us
    all_to_all x4 -> x0, waiting for transfers between devices: 928 us -> none  [the longest x2 614 us: return_rows(): lax.all_to_all(shaped, ('expert', 'hidden'), split_axis=0, concat_axis=0,...]
    pallas_call x0 -> x3, Pallas kernels: none -> 248 us  [the longest x1 223 us: on_device(): out = lax.switch(level[0], branches, *operands)]
    all_to_all x4 -> x0, starting transfers between devices: 168 us -> none  [the longest x2 120 us: return_rows(): lax.all_to_all(shaped, ('expert', 'hidden'), split_axis=0, concat_axis=0,...]
    psum x1 -> x0, blocking collectives: 115 us -> none  [on_device(): lax.psum((gain_part, router_part), ('dp', 'expert', 'hidden'))]
    dot_general x9 -> x0, matrix products: 109 us -> none  [the longest x1 23.1 us: on_device(): jnp.dot(pre_grad, first_weight.T, preferred_element_type=jnp.float32)]
    reduce_sum x7 -> x0, other arithmetic: 19.9 us -> none  [the longest x2 15.6 us: return_rows(): jnp.sum(returned.reshape(expert_count, hidden_count, capacity, width), ax...]
  transfers between devices with their start and end apart: 5 -> 0, of which waited for: 4 -> 0; matrix products, arithmetic and copies ran while one was open for 7% -> 0% of each run, Pallas kernels for 0% -> 0%
where the time goes in v2:
time: 255 us; the launch traced here: 253 us
  Pallas kernels  248 us (97%)
    pallas_call x1, Pallas kernels, on_device(): out = lax.switch(level[0], branches, *operands)  223 us
    pallas_call x1, Pallas kernels, on_device(): pl.pallas_call(functools.partial(prologue_kernel, experts, pairs, halves,...  15.1 us
    pallas_call x1, Pallas kernels, on_device(): pl.pallas_call(functools.partial(finish_kernel, experts), grid=(steps,),...  10.3 us

profile of v2, /device:TPU:0, one launch (start us, length us, event | category | flops | bytes accessed | tf_op | source)
XLA Modules:
  0.0 252.6 jit_solution(16793059635985566875)
XLA Ops:
  0.6 0.0 copy-start
  0.6 1.4 broadcast_in_dim.9.gain_ref
  2.1 15.1 %shard_map.118 = (bf16[1024,1152]{1,0:T(8,128)(2,1)}, bf16[1024,1152]{1,0:T(8,128)(2,1)}, f32[512,128]{1,0:T(8,128)S(1)}, s32[1]{0:T(128)}) custom-call(bf16[512,1152]{1,0:T(8,128)(2,1)} %x_hbm.1, s32[1,512]{1,0:T(1,128)} %bitcast.24, bf16[1,1152]{1,0:T(2,128)(2,1)} %broadcast_in_dim.9.gain_ref, bf16[4,1152]{1,0:T(4,128)(2,1)} %bitcast.18, ...), custom_call_target="tpu_custom_call" | custom-call | tf_op jit(solution)/shard_map/pallas_call | solution.py:740
  17.9 0.0 copy-done
  17.9 223.1 %conditional.1 = ((bf16[512,1152]{1,0:T(8,128)(2,1)}, f32[512,1152]{1,0:T(8,128)}, f32[8,1152]{1,0:T(8,128)}, bf16[1152,768]{1,0:T(8,128)(2,1)}, bf16[768,1152]{...) conditional(s32[]{:T(128)} %bitcast.2, ...), branch_computations={%region_0.0_spmd, %region_1.0_spmd, %region_2.0_spmd, %region_3.0_... | conditional | bytes 8 | solution.py:822
  18.1 222.5 %branch_2_fun.1 = (bf16[512,1152]{1,0:T(8,128)(2,1)}, f32[512,1152]{1,0:T(8,128)}, f32[8,1152]{1,0:T(8,128)}, bf16[1152,768]{1,0:T(8,128)(2,1)}, bf16[768,1152]{...) custom-call(bf16[512,1152]{1,0:T(8,128)(2,1)} %get-tuple-element.108.x_hbm, ...), custom_call_target="tpu_custom_call" | custom-call | tf_op jit(solution)/shard_map/cond/branch_2_fun/pallas_call | solution.py:822
  241.0 10.3 %shard_map.119 = (bf16[512,1152]{1,0:T(8,128)(2,1)}, f32[512,1152]{1,0:T(8,128)}, f32[1,1152]{1,0:T(1,128)}, f32[4,1152]{1,0:T(4,128)}, f32[1152,768]{1,0:T(8,128)}, /*index=5*/f32[768,1152]{1,0:T(8,128)}) custom-call(bf16[512,1152]{1,0:T(8,128)(2,1)} %get-tuple-element.162.act, f32[512,1152]{1,0:T(8,128)} %get-tuple-element.163.ig, ...), custom_call_target="tpu_custom_call" | custom-call | tf_op jit(solution)/shard_map/pallas_call | solution.py:846
  251.3 1.3 reduce
Async XLA Ops:
  0.6 17.2 %copy-start = (bf16[1,1152,768]{2,1,0:T(8,128)(2,1)S(1)}, bf16[1,1152,768]{2,1,0:T(8,128)(2,1)}, u32[]{:S(2)}) copy-start(bf16[1,1152,768]{2,1,0:T(8,128)(2,1)} %param.16) | copy-start | bytes 5308420

commit v3 on v2

--- a/solution.py
+++ b/solution.py
@@ -29,6 +29,10 @@
     return out
 
 
+def one_row(ref):
+    return jnp.concatenate([ref[i:i + 1, :].astype(F32) for i in range(ref.shape[0])], axis=1)
+
+
 def contract(a, b, left, right, **kwargs):
     return lax.dot_general(a, b, (((left,), (right,)), ((), ())), preferred_element_type=F32, **kwargs)
 
@@ -81,7 +85,7 @@
     experts, pairs, halves, cold,
     x_hbm, route_ref, gain_ref, router_ref, cot_hbm,
     bn_out, bg_out, aux_ref, level_ref,
-    x_ref, cot_ref, place, router, ranks, stage, counts, count_in, line_in, send, recv, load, local,
+    x_ref, cot_ref, place, router, ranks, marks, stage, counts, count_in, line_in, send, recv, load, local,
 ):
     tokens, width = x_ref.shape
     cap = bn_out.shape[0] // experts
@@ -97,12 +101,19 @@
     chosen = jnp.transpose(jnp.broadcast_to(route_ref[...].astype(F32), (TILE, tokens)))
     onehot = (chosen.astype(jnp.int32) == lane).astype(F32)
     counts[...] = jnp.broadcast_to(jnp.sum(onehot, axis=0, keepdims=True), (8, TILE))
-    before = (
-        lax.broadcasted_iota(jnp.int32, (tokens, tokens), 1) < lax.broadcasted_iota(jnp.int32, (tokens, tokens), 0)
-    ).astype(BF16)
-    rank = jnp.sum(dot_nn(before, onehot.astype(BF16)) * onehot, axis=1, keepdims=True)
     ranks[0] = chosen
-    ranks[1] = chosen * cap + rank
+    marks[...] = onehot.astype(BF16)
+
+    @pl.loop(0, tokens // TILE)
+    def _(i):
+        rows = pl.ds(pl.multiple_of(i * TILE, TILE), TILE)
+        before = (
+            lax.broadcasted_iota(jnp.int32, (TILE, tokens), 1)
+            < lax.broadcasted_iota(jnp.int32, (TILE, tokens), 0) + i * TILE
+        ).astype(BF16)
+        rank = jnp.sum(dot_nn(before, marks[...]) * marks[rows, :].astype(F32), axis=1, keepdims=True)
+        ranks[1, rows, :] = ranks[0, rows, :] * cap + rank
+
     router[...] = jnp.zeros_like(router)
     router[pl.ds(0, experts), :] = router_ref[...]
 
@@ -129,7 +140,7 @@
         rows = pl.ds(pl.multiple_of(i * TILE, TILE), TILE)
         x = x_ref[rows, :].astype(F32)
         inverse = lax.rsqrt(jnp.mean(x * x, axis=1, keepdims=True) + EPSILON)
-        low = (x * inverse * gain_ref[...].astype(F32)).astype(BF16)
+        low = (x * inverse * one_row(gain_ref)).astype(BF16)
         x_ref[rows, :] = low
         lanes = lax.broadcasted_iota(jnp.int32, (TILE, TILE), 1)
         expert, slot = ranks[0, rows, :], ranks[1, rows, :]
@@ -143,8 +154,11 @@
         aux = jnp.where(lanes == experts + 2, slot, aux)
         aux_ref[rows, :] = jnp.where(lanes == experts + 3, expert, aux)
         slot_int = slot.astype(jnp.int32)
-        for j in range(experts * cap // TILE):
-            place[rows, pl.ds(j * TILE, TILE)] = (slot_int == lanes + j * TILE).astype(BF16)
+
+        @pl.loop(0, experts * cap // TILE)
+        def _(j):
+            at = pl.ds(pl.multiple_of(j * TILE, TILE), TILE)
+            place[rows, at] = (slot_int == lanes + j * TILE).astype(BF16)
 
     most = counts[...]
     for i in range(1, here):
@@ -246,12 +260,10 @@
     def z_start(t, k):
         sized(flip(z, k, experts), lambda rows: z_copy(t, k, rows).start())
 
-    early = max(1, experts - 1)
-
-    @pl.loop(1, early)
-    def _(n):
+    order = sorted(range(1, experts), key=lambda k: (k != experts - 1, k))
+    for k in order:
         for t in (0, 1):
-            z_start(t, turn_k(early - n))
+            z_start(t, k)
 
     mats = ((win_hbm, w_in), (wout_hbm, w_out))
 
@@ -326,34 +338,25 @@
     for t in (0, 1):
         sized(z, lambda rows: own_local(t, rows).wait())
 
-    for which in (0, 1):
-        @pl.when(parity == which)
-        def _():
-            @pl.loop(0, weight_parts)
-            def _(part):
-                weight_copy(which, part).wait_recv()
-                weight_pass(which, part).start()
-
-    final = turn_k(experts - 1)
-    if experts > 1:
-        for t in (0, 1):
-            if experts > 2:
-                k = turn_k(experts - 2)
-                sized(flip(z, k, experts), lambda rows: z_copy(t, k, rows).wait_send())
-            z_start(t, final)
-
-    for which in (0, 1):
-        @pl.when(parity == which)
-        def _():
-            @pl.loop(0, weight_parts)
-            def _(part):
-                weight_pass(1 - which, part).wait_recv()
-                weight_copy(which, part).wait_send()
-                weight_pass(which, part).wait_send()
-
-    def token_block(turn):
+    def other_weights():
+        for which in (0, 1):
+            @pl.when(parity == which)
+            def _():
+                @pl.loop(0, weight_parts)
+                def _(part):
+                    weight_copy(which, part).wait_recv()
+                    weight_pass(which, part).start()
+
+                @pl.loop(0, weight_parts)
+                def _(part):
+                    weight_pass(1 - which, part).wait_recv()
+                    weight_copy(which, part).wait_send()
+                    weight_pass(which, part).wait_send()
+
+    per_half = hid // hidden_tile
+
+    def rows_in(turn):
         k = turn_k(turn)
-        source = flip(z, k, experts)
 
         @pl.when(turn > 0)
         def _():
@@ -369,30 +372,24 @@
 
         for t in (0, 1):
             sized(z, lambda rows: pair_copy(t, k, rows).wait_recv())
+
+    def token_block(turn, first, last):
+        source = flip(z, turn_k(turn), experts)
         chunk = pl.ds(pl.multiple_of(source * 2 * cap, 2 * cap), 2 * cap)
-        per_half = hid // hidden_tile
-
-        @pl.loop(0, 2 * per_half)
+
+        @pl.loop(first, last)
         def _(j):
             half = lax.div(j, per_half)
             cols = pl.ds(pl.multiple_of(lax.rem(j, per_half) * hidden_tile, hidden_tile), hidden_tile)
             pre = dot_nn(xs[chunk, :], w_in[half, :, cols])
             back = dot_nt(gs[chunk, :], w_out[half, cols, :])
             square = pre * pre
-            curve = jnp.tanh(C0 * pre * (1.0 + C1 * square))
-            low_half = 0.5 * (1.0 + curve)
-            slope = low_half + (0.5 * C0) * pre * (1.0 - curve * curve) * (1.0 + (3.0 * C1) * square)
+            curve = jnp.tanh(pre * (C0 + (C0 * C1) * square))
+            low_half = 0.5 + 0.5 * curve
+            slope = low_half + pre * (1.0 - curve * curve) * (0.5 * C0 + (1.5 * C0 * C1) * square)
             at = pl.ds(pl.multiple_of(j * hidden_tile, hidden_tile), hidden_tile)
             hs[chunk, at] = (pre * low_half).astype(BF16)
             ps[chunk, at] = (back * slope).astype(BF16)
-
-            @pl.when((turn == experts - 1) & (j == 1))
-            def _():
-                pl.semaphore_wait(all_in, experts - 1)
-
-                @pl.loop(1, experts - 1)
-                def _(earlier):
-                    held(earlier)
 
     def rs_copy(t, k, slot):
         return remote(
@@ -422,12 +419,13 @@
     def token_sums(turn):
         k = turn_k(turn)
         source = flip(z, k, experts)
-        slot = lax.rem(turn, 2)
-
-        @pl.when(turn >= 2)
+        place_in = lax.rem(turn + experts - 1, experts)
+        slot = lax.rem(place_in, 2)
+
+        @pl.when(place_in >= 2)
         def _():
             for t in (0, 1):
-                rs_copy(t, turn_k(turn - 2), slot).wait_send()
+                rs_copy(t, turn_k(place_in - 1), slot).wait_send()
 
         @pl.loop(0, 2)
         def _(mine):
@@ -436,8 +434,12 @@
                 ((hs, w_out, dot_nn, acc_n), (ps, w_in, dot_nt, acc_g))
             ):
                 acc = acc.at[pl.ds(0, cap)]
-                acc[...] = dot(values[rows, pl.ds(0, hid)], weights[0])
-                acc[...] += dot(values[rows, pl.ds(hid, hid)], weights[1])
+                acc[...] = jnp.zeros_like(acc)
+
+                @pl.loop(0, 2)
+                def _(half):
+                    cols = pl.ds(pl.multiple_of(half * hid, hid), hid)
+                    acc[...] += dot(values[rows, cols], weights[half])
 
                 @pl.when(mine == 0)
                 def _():
@@ -512,8 +514,12 @@
         @pl.loop(0, 3)
         def _(n):
             cols = pl.ds(pl.multiple_of(n * (width // 3), width // 3), width // 3)
-            got_n[:, cols] = dot_nn(place[...], ret_n[:, cols]).astype(BF16)
-            got_g[:, cols] = dot_nn(place[...], ret_g[:, cols]).astype(BF16)
+
+            @pl.loop(0, tokens // TILE)
+            def _(m):
+                rows = pl.ds(pl.multiple_of(m * TILE, TILE), TILE)
+                got_n[rows, cols] = dot_nn(place[rows, :], ret_n[:, cols]).astype(BF16)
+                got_g[rows, cols] = dot_nn(place[rows, :], ret_g[:, cols]).astype(BF16)
 
     def out_copy(t, i):
         rows = pl.ds(pl.multiple_of(i * SMALL, SMALL), SMALL)
@@ -529,7 +535,7 @@
         expert_g = got_g[rows, :].astype(F32)
         x = x_ref[rows, :].astype(F32)
         up = cot_ref[rows, :].astype(F32)
-        gain = gain_ref[...].astype(F32)
+        gain = one_row(gain_ref)
         hits = (chosen == lax.broadcasted_iota(jnp.int32, (SMALL, experts), 1)).astype(F32)
         act_ref[rows, :] = (x + g * expert_out).astype(BF16)
         out_copy(0, i).start()
@@ -601,62 +607,97 @@
         def _(i):
             red_line_copy(i).start()
 
-    def grad_step(step):
-        half = jnp.where(step < grad_parts, 1, 0)
-        i = lax.rem(step, grad_parts)
-        for t in (0, 1):
-            weight_grad(t, i, half)
-            out, got = ((g_in, y_in), (g_out, y_out))[t]
-
-            @pl.when(half == 1)
+    plans = (((1, 0), (0, 0), (1, 1), (1, 2), (0, 1), (0, 2)), ((1, 0), (1, 1), (0, 0), (1, 2), (0, 1), (0, 2)))
+    late_steps = len(plans[0])
+
+    def planned(t, step, what):
+        return sum(jnp.where(step == n, plan[what], 0) for n, plan in enumerate(plans[t]))
+
+    def grad_form(t, step):
+        weight_grad(t, planned(t, step, 1), planned(t, step, 0))
+
+    def grad_pass(t, step):
+        half, i = planned(t, step, 0), planned(t, step, 1)
+        out, got = ((g_in, y_in), (g_out, y_out))[t]
+
+        @pl.when(half == 1)
+        def _():
+            out[grad_span(t, i), :] = accs[t][...].astype(BF16)
+
+            @pl.loop(0, subs[t])
+            def _(sub):
+                y_copy(t, i, sub).start()
+
+        @pl.when(half == 0)
+        def _():
+            @pl.loop(0, subs[t])
+            def _(sub):
+                if t:
+                    @pl.when((step == late_steps - 1) & (sub == subs[1] - 1))
+                    def _():
+                        token_results()
+
+                span = grad_span(t, i, sub)
+                y_copy(t, i, sub).wait_recv()
+                mine = accs[t][pl.ds(pl.multiple_of(sub * PIECE, PIECE), PIECE), :]
+                got[span, :] = (mine + got[span, :].astype(F32)).astype(BF16)
+                if pairs == 2:
+                    d_copy(t, i, sub).start()
+                d_local(t, i, sub).start()
+
+    @pl.loop(0, experts + 1 + late_steps)
+    def _(step):
+        late = step - experts - 1
+
+        @pl.when(late >= 0)
+        def _():
+            grad_form(0, late)
+
+        @pl.when(((step > 2) & (step <= experts)) | (late == 1) | (late == 3))
+        def _():
+            token_sums(jnp.where(step <= experts, step - 2, jnp.where(late == 1, experts - 1, 0)))
+
+        @pl.when(late == 1)
+        def _():
+            back_start(experts - 1)
+
+        if hot is not None:
+            @pl.when((step > 2) & (step <= experts) & (z == hot))
             def _():
-                out[grad_span(t, i), :] = accs[t][...].astype(BF16)
-
-                @pl.loop(0, subs[t])
-                def _(sub):
-                    y_copy(t, i, sub).start()
-
-            if t:
-                @pl.when(step == 2 * grad_parts - 1)
-                def _():
-                    token_results()
-
-            @pl.when(half == 0)
+                back_start(step - 2)
+
+        @pl.when(late >= 0)
+        def _():
+            grad_pass(0, late)
+
+            @pl.when(late == 0)
             def _():
-                @pl.loop(0, subs[t])
-                def _(sub):
-                    span = grad_span(t, i, sub)
-                    y_copy(t, i, sub).wait_recv()
-                    mine = accs[t][pl.ds(pl.multiple_of(sub * PIECE, PIECE), PIECE), :]
-                    got[span, :] = (mine + got[span, :].astype(F32)).astype(BF16)
-                    if pairs == 2:
-                        d_copy(t, i, sub).start()
-                    d_local(t, i, sub).start()
-
-    @pl.loop(0, experts + 2 * grad_parts)
-    def _(step):
-        late = experts + 1
-
-        @pl.when(((step > 0) & (step < experts)) | (step == late))
-        def _():
-            token_sums(jnp.where(step < experts, step, experts) - 1)
-
-        @pl.when(step == late)
-        def _():
-            back_start(experts - 1)
-
-        if hot is not None:
-            @pl.when((step > 1) & (step < experts) & (z == hot))
-            def _():
-                back_start(step - 1)
-
-        @pl.when(step < experts)
-        def _():
-            token_block(step)
-
-        @pl.when(step >= experts)
-        def _():
-            grad_step(step - experts)
+                pl.semaphore_wait(all_in, experts - 1)
+
+                @pl.loop(1, experts - 1)
+                def _(earlier):
+                    held(earlier)
+
+            grad_form(1, late)
+            grad_pass(1, late)
+
+        @pl.when(step == 1)
+        def _():
+            other_weights()
+
+        turn = jnp.where(step < 2, 0, jnp.where(step <= experts, step - 1, experts - 1))
+
+        @pl.when((step != 1) & (step <= experts))
+        def _():
+            rows_in(turn)
+
+        @pl.when(step <= experts + 1)
+        def _():
+            token_block(
+                turn,
+                jnp.where((step == 1) | (step == experts), per_half, 0),
+                jnp.where((step == 0) | (step == experts + 1), per_half, 2 * per_half),
+            )
 
     plane_sum()
 
@@ -673,18 +714,13 @@
     def _(turn):
         k = turn_k(turn)
         for t in (0, 1):
-            if experts > 2:
-                @pl.when(turn != experts - 2)
-                def _():
-                    sized(flip(z, k, experts), lambda rows: z_copy(t, k, rows).wait_send())
-            else:
-                sized(flip(z, k, experts), lambda rows: z_copy(t, k, rows).wait_send())
+            sized(flip(z, k, experts), lambda rows: z_copy(t, k, rows).wait_send())
             sized(z, lambda rows: pair_copy(t, k, rows).wait_send())
             sized(z, lambda rows: back_copy(t, k, rows).wait_send())
     for t in (0, 1):
         sized(z, lambda rows: own_pair(t, rows).wait_send())
-        for turn in range(max(0, experts - 2), experts):
-            rs_copy(t, turn_k(turn), turn % 2).wait_send()
+        for place_in in range(max(0, experts - 2), experts):
+            rs_copy(t, turn_k((place_in + 1) % experts), place_in % 2).wait_send()
 
     @pl.loop(0, tokens // SMALL)
     def _(i):
@@ -710,7 +746,8 @@
 
     @pl.when(pl.program_id(0) == 0)
     def _():
-        gain_out[...] = red[pl.ds(experts, 1), :]
+        for i in range(gain_out.shape[0]):
+            gain_out[i:i + 1, :] = red[experts:experts + 1, i * TILE:(i + 1) * TILE]
         router_out[...] = red[pl.ds(0, experts), :]
 
 
@@ -723,7 +760,7 @@
     hid = w_in.shape[2]
     cold = 16 * (-(-11 * cap // 256))
     hidden_tile = 256
-    weight_parts, grad_parts = 4, 3
+    weight_parts, grad_parts = 12, 3
     grad_pieces = max(width, hid) // PIECE
     slot_rows = experts * cap
     both = 2 * slot_rows
@@ -734,7 +771,7 @@
     sem = pltpu.SemaphoreType.DMA
     shape = jax.ShapeDtypeStruct
     params = functools.partial(pltpu.CompilerParams, has_side_effects=True, vmem_limit_bytes=62 * 1024 * 1024)
-    gain_row = norm_gain[None, :]
+    gain_row = norm_gain.reshape(width // TILE, TILE)
     router_rows = router_weight.T
 
     bn, bg, aux, level = pl.pallas_call(
@@ -753,6 +790,7 @@
             pltpu.VMEM((rows, slot_rows), BF16),
             pltpu.VMEM((TILE, width), BF16),
             pltpu.VMEM((2, rows, TILE), F32),
+            pltpu.VMEM((rows, TILE), BF16),
             pltpu.VMEM((2, slot_rows, width), BF16),
             pltpu.VMEM((8, TILE), F32),
             pltpu.VMEM((pairs * halves, 8, TILE), F32),
@@ -827,7 +865,7 @@
         first, second = lax.psum((ga_in.astype(F32), ga_out.astype(F32)), "dp")
         return act, ig, red[experts], red[:experts].T, first[None], second[None]
 
-    steps = 8
+    steps = 2
 
     def blocked(array):
         return pl.BlockSpec((array.shape[0] // steps, array.shape[1]), lambda i: (i, 0))
@@ -838,7 +876,7 @@
     outs = [
         shape((rows, width), BF16),
         shape((rows, width), F32),
-        shape((1, width), F32),
+        shape((width // TILE, TILE), F32),
         shape((experts, width), F32),
         shape((width, hid), F32),
         shape((hid, width), F32),
@@ -850,7 +888,7 @@
         in_specs=[blocked(act), blocked(ig), whole(red)] + [blocked(a) for a in (ga_in, ga_out, gb_in, gb_out)],
         out_specs=[blocked(outs[0]), blocked(outs[1]), whole(outs[2]), whole(outs[3]), blocked(outs[4]), blocked(outs[5])],
     )(act, ig, red, ga_in, ga_out, gb_in, gb_out)
-    return act, ig, gain_grad[0], router_grad.T, first[None], second[None]
+    return act, ig, gain_grad.reshape(width), router_grad.T, first[None], second[None]
 
 
 def solution(mesh):

time: 255 us -> 225 us (0.88); the launches traced: 253 us -> 226 us
  Pallas kernels: 248 us -> 224 us
    pallas_call x1, Pallas kernels: 223 us -> 201 us  [on_device(): out = lax.switch(level[0], branches, *operands)]
    pallas_call x1, Pallas kernels: 10.3 us -> 7.64 us  [on_device(): pl.pallas_call(functools.partial(finish_kernel, experts), grid=(steps,),...]
where the time goes in v3:
time: 225 us; the launch traced here: 226 us
  Pallas kernels  224 us (100%)
    pallas_call x1, Pallas kernels, on_device(): out = lax.switch(level[0], branches, *operands)  201 us
    pallas_call x1, Pallas kernels, on_device(): pl.pallas_call(functools.partial(prologue_kernel, experts, pairs, halves,...  15.3 us
    pallas_call x1, Pallas kernels, on_device(): pl.pallas_call(functools.partial(finish_kernel, experts), grid=(steps,),...  7.64 us

profile of v3, /device:TPU:0, one launch (start us, length us, event | category | flops | bytes accessed | tf_op | source)
XLA Modules:
  0.0 226.2 jit_solution(14676433822782145327)
XLA Ops:
  0.6 0.0 copy-start
  0.6 15.3 %shard_map.118 = (bf16[1024,1152]{1,0:T(8,128)(2,1)}, bf16[1024,1152]{1,0:T(8,128)(2,1)}, f32[512,128]{1,0:T(8,128)S(1)}, s32[1]{0:T(128)}) custom-call(bf16[512,1152]{1,0:T(8,128)(2,1)} %x_hbm.1, s32[1,512]{1,0:T(1,128)} %bitcast.32, bf16[9,128]{1,0:T(8,128)(2,1)} %bitcast.26, bf16[4,1152]{1,0:T(4,128)(2,1)} %bitcast.20, bf16[512,1152]{1,0:T(8,128)(2,1)} %cot_hbm.1), custom_call_target="tpu_custom_call" | custom-call | tf_op jit(solution)/shard_map/pallas_call | solution.py:777
  16.5 0.0 copy-done
  16.5 201.9 %conditional.1 = ((bf16[512,1152]{1,0:T(8,128)(2,1)}, f32[512,1152]{1,0:T(8,128)}, f32[8,1152]{1,0:T(8,128)}, bf16[1152,768]{1,0:T(8,128)(2,1)}, bf16[768,1152]{...) conditional(s32[]{:T(128)} %bitcast.3, ...), branch_computations={%region_0.0_spmd, %region_1.0_spmd, %region_2.0_spmd, %region_3.0_... | conditional | bytes 8 | solution.py:860
  16.7 201.0 %branch_3_fun.1 = (bf16[512,1152]{1,0:T(8,128)(2,1)}, f32[512,1152]{1,0:T(8,128)}, f32[8,1152]{1,0:T(8,128)}, bf16[1152,768]{1,0:T(8,128)(2,1)}, bf16[768,1152]{...) custom-call(bf16[512,1152]{1,0:T(8,128)(2,1)} %get-tuple-element.117.x_hbm, ...), custom_call_target="tpu_custom_call" | custom-call | tf_op jit(solution)/shard_map/cond/branch_3_fun/pallas_call | solution.py:860
  218.4 7.6 %shard_map.119 = (bf16[512,1152]{1,0:T(8,128)(2,1)}, f32[512,1152]{1,0:T(8,128)}, f32[9,128]{1,0:T(8,128)}, f32[4,1152]{1,0:T(4,128)}, f32[1152,768]{1,0:T(8,128)}, /*index=5*/f32[768,1152]{1,0:T(8,128)}) custom-call(bf16[512,1152]{1,0:T(8,128)(2,1)} %get-tuple-element.162.act, f32[512,1152]{1,0:T(8,128)} %get-tuple-element.163.ig, ...), custom_call_target="tpu_custom_call" | custom-call | tf_op jit(solution)/shard_map/pallas_call | solution.py:884
Async XLA Ops:
  0.6 15.8 %copy-start = (bf16[1,1152,768]{2,1,0:T(8,128)(2,1)S(1)}, bf16[1,1152,768]{2,1,0:T(8,128)(2,1)}, u32[]{:S(2)}) copy-start(bf16[1,1152,768]{2,1,0:T(8,128)(2,1)} %param.16) | copy-start | bytes 5308420

commit v4 on v3

--- a/solution.py
+++ b/solution.py
@@ -214,7 +214,7 @@
     xs, gs, hs, ps, g_in, g_out, y_in, y_out,
     rs_send, rs_n, rs_g, acc_n, acc_g, acc_in, logits, ret_n, ret_g, total, red_plane, red_line,
     w_send, w_recv, wf_send, wf_recv, z_send, z_recv, f_send, f_recv, r_send, r_recv,
-    b_send, b_recv, y_send, y_recv, d_send, d_recv, red_send, red_recv, load, local, out_sem, all_in,
+    b_send, b_recv, y_send, y_recv, d_send, d_recv, red_send, red_recv, load, local, out_sem,
 ):
     tokens, width = x_ref.shape
     hid = w_in.shape[2]
@@ -363,12 +363,6 @@
             for t in (0, 1):
                 sized(z, lambda rows: z_copy(t, k, rows).wait_recv())
                 sized(z, lambda rows: pair_copy(t, k, rows).start())
-
-        @pl.when(turn == experts - 1)
-        def _():
-            @pl.loop(1, experts)
-            def _(i):
-                pl.semaphore_signal(all_in, inc=1, device_id=line_peer(i, experts), device_id_type=MESH)
 
         for t in (0, 1):
             sized(z, lambda rows: pair_copy(t, k, rows).wait_recv())
@@ -607,7 +601,7 @@
         def _(i):
             red_line_copy(i).start()
 
-    plans = (((1, 0), (0, 0), (1, 1), (1, 2), (0, 1), (0, 2)), ((1, 0), (1, 1), (0, 0), (1, 2), (0, 1), (0, 2)))
+    plans = (((1, 0), (0, 0), (1, 1), (1, 2), (0, 1), (0, 2)), ((1, 0), (1, 1), (0, 0), (0, 1), (1, 2), (0, 2)))
     late_steps = len(plans[0])
 
     def planned(t, step, what):
@@ -670,14 +664,6 @@
         def _():
             grad_pass(0, late)
 
-            @pl.when(late == 0)
-            def _():
-                pl.semaphore_wait(all_in, experts - 1)
-
-                @pl.loop(1, experts - 1)
-                def _(earlier):
-                    held(earlier)
-
             grad_form(1, late)
             grad_pass(1, late)
 
@@ -698,6 +684,12 @@
                 jnp.where((step == 1) | (step == experts), per_half, 0),
                 jnp.where((step == 0) | (step == experts + 1), per_half, 2 * per_half),
             )
+
+        @pl.when(step == experts)
+        def _():
+            @pl.loop(1, experts - 1)
+            def _(earlier):
+                held(earlier)
 
     plane_sum()
 
@@ -849,7 +841,6 @@
                 sem((2, experts)), sem((2, experts)), sem((2, experts)), sem((2, experts)),
                 sem((2, grad_pieces)), sem((2, grad_pieces)), sem((2, grad_pieces)), sem((2, grad_pieces)),
                 sem((peers,)), sem((peers,)), sem((7,)), sem((2, grad_pieces)), sem((2, rows // SMALL)),
-                pltpu.SemaphoreType.REGULAR,
             ],
             compiler_params=params(collective_id=1 + (experts if hot is None else hot)),
         )

time: 225 us -> 223 us (level)
  Pallas kernels: 224 us -> 221 us
    pallas_call x1, Pallas kernels: 201 us -> 198 us  [on_device(): out = lax.switch(level[0], branches, *operands)]
where the time goes in v4:
time: 223 us
  Pallas kernels  221 us (99%)
    pallas_call x1, Pallas kernels, on_device(): out = lax.switch(level[0], branches, *operands)  198 us
    pallas_call x1, Pallas kernels, on_device(): pl.pallas_call(functools.partial(prologue_kernel, experts, pairs, halves,...  15.3 us
    pallas_call x1, Pallas kernels, on_device(): pl.pallas_call(functools.partial(finish_kernel, experts), grid=(steps,),...  7.64 us

profile of v4, /device:TPU:0, one launch (start us, length us, event | category | flops | bytes accessed | tf_op | source)
XLA Modules:
  0.0 222.9 jit_solution(14193348482046546255)
XLA Ops:
  0.6 0.0 copy-start
  0.6 15.3 %shard_map.118 = (bf16[1024,1152]{1,0:T(8,128)(2,1)}, bf16[1024,1152]{1,0:T(8,128)(2,1)}, f32[512,128]{1,0:T(8,128)S(1)}, s32[1]{0:T(128)}) custom-call(bf16[512,1152]{1,0:T(8,128)(2,1)} %x_hbm.1, s32[1,512]{1,0:T(1,128)} %bitcast.32, bf16[9,128]{1,0:T(8,128)(2,1)} %bitcast.26, bf16[4,1152]{1,0:T(4,128)(2,1)} %bitcast.20, bf16[512,1152]{1,0:T(8,128)(2,1)} %cot_hbm.1), custom_call_target="tpu_custom_call" | custom-call | tf_op jit(solution)/shard_map/pallas_call | solution.py:769
  16.5 0.0 copy-done
  16.5 198.5 %conditional.1 = ((bf16[512,1152]{1,0:T(8,128)(2,1)}, f32[512,1152]{1,0:T(8,128)}, f32[8,1152]{1,0:T(8,128)}, bf16[1152,768]{1,0:T(8,128)(2,1)}, bf16[768,1152]{...) conditional(s32[]{:T(128)} %bitcast.3, ...), branch_computations={%region_0.0_spmd, %region_1.0_spmd, %region_2.0_spmd, %region_3.0_... | conditional | bytes 8 | solution.py:851
  16.7 197.6 %branch_3_fun.1 = (bf16[512,1152]{1,0:T(8,128)(2,1)}, f32[512,1152]{1,0:T(8,128)}, f32[8,1152]{1,0:T(8,128)}, bf16[1152,768]{1,0:T(8,128)(2,1)}, bf16[768,1152]{...) custom-call(bf16[512,1152]{1,0:T(8,128)(2,1)} %get-tuple-element.117.x_hbm, ...), custom_call_target="tpu_custom_call" | custom-call | tf_op jit(solution)/shard_map/cond/branch_3_fun/pallas_call | solution.py:851
  215.0 7.6 %shard_map.119 = (bf16[512,1152]{1,0:T(8,128)(2,1)}, f32[512,1152]{1,0:T(8,128)}, f32[9,128]{1,0:T(8,128)}, f32[4,1152]{1,0:T(4,128)}, f32[1152,768]{1,0:T(8,128)}, /*index=5*/f32[768,1152]{1,0:T(8,128)}) custom-call(bf16[512,1152]{1,0:T(8,128)(2,1)} %get-tuple-element.162.act, f32[512,1152]{1,0:T(8,128)} %get-tuple-element.163.ig, ...), custom_call_target="tpu_custom_call" | custom-call | tf_op jit(solution)/shard_map/pallas_call | solution.py:875
Async XLA Ops:
  0.6 15.8 %copy-start = (bf16[1,1152,768]{2,1,0:T(8,128)(2,1)S(1)}, bf16[1,1152,768]{2,1,0:T(8,128)(2,1)}, u32[]{:S(2)}) copy-start(bf16[1,1152,768]{2,1,0:T(8,128)(2,1)} %param.16) | copy-start | bytes 5308420

commit v5 on v4

--- a/solution.py
+++ b/solution.py
@@ -101,6 +101,21 @@
     chosen = jnp.transpose(jnp.broadcast_to(route_ref[...].astype(F32), (TILE, tokens)))
     onehot = (chosen.astype(jnp.int32) == lane).astype(F32)
     counts[...] = jnp.broadcast_to(jnp.sum(onehot, axis=0, keepdims=True), (8, TILE))
+    here = pairs * halves
+
+    def plane_copy(i):
+        return remote(counts, count_in.at[i], send.at[i], recv.at[i], plane_peer(i, pairs, halves))
+
+    def line_copy(i):
+        at = here - 1 + i
+        return remote(count_in.at[0], line_in.at[i], send.at[at], recv.at[at], line_peer(i, experts))
+
+    wait_all(pairs, experts, halves)
+
+    @pl.loop(1, here)
+    def _(i):
+        plane_copy(i).start()
+
     ranks[0] = chosen
     marks[...] = onehot.astype(BF16)
 
@@ -116,21 +131,6 @@
 
     router[...] = jnp.zeros_like(router)
     router[pl.ds(0, experts), :] = router_ref[...]
-
-    here = pairs * halves
-
-    def plane_copy(i):
-        return remote(counts, count_in.at[i], send.at[i], recv.at[i], plane_peer(i, pairs, halves))
-
-    def line_copy(i):
-        at = here - 1 + i
-        return remote(count_in.at[0], line_in.at[i], send.at[at], recv.at[at], line_peer(i, experts))
-
-    wait_all(pairs, experts, halves)
-
-    @pl.loop(1, here)
-    def _(i):
-        plane_copy(i).start()
 
     for copy in loads:
         copy.wait()

time: 223 us -> 222 us (level)
  no operation moved by 1% of the time
where the time goes in v5:
time: 222 us; the launch traced here: 221 us
  Pallas kernels  219 us (99%)
    pallas_call x1, Pallas kernels, on_device(): out = lax.switch(level[0], branches, *operands)  196 us
    pallas_call x1, Pallas kernels, on_device(): pl.pallas_call(functools.partial(prologue_kernel, experts, pairs, halves,...  15.3 us
    pallas_call x1, Pallas kernels, on_device(): pl.pallas_call(functools.partial(finish_kernel, experts), grid=(steps,),...  7.64 us

profile of v5, /device:TPU:0, one launch (start us, length us, event | category | flops | bytes accessed | tf_op | source)
XLA Modules:
  0.0 221.3 jit_solution(4085150807740339736)
XLA Ops:
  0.6 0.0 copy-start
  0.6 15.3 %shard_map.118 = (bf16[1024,1152]{1,0:T(8,128)(2,1)}, bf16[1024,1152]{1,0:T(8,128)(2,1)}, f32[512,128]{1,0:T(8,128)S(1)}, s32[1]{0:T(128)}) custom-call(bf16[512,1152]{1,0:T(8,128)(2,1)} %x_hbm.1, s32[1,512]{1,0:T(1,128)} %bitcast.32, bf16[9,128]{1,0:T(8,128)(2,1)} %bitcast.26, bf16[4,1152]{1,0:T(4,128)(2,1)} %bitcast.20, bf16[512,1152]{1,0:T(8,128)(2,1)} %cot_hbm.1), custom_call_target="tpu_custom_call" | custom-call | tf_op jit(solution)/shard_map/pallas_call | solution.py:769
  16.5 0.0 copy-done
  16.5 196.9 %conditional.1 = ((bf16[512,1152]{1,0:T(8,128)(2,1)}, f32[512,1152]{1,0:T(8,128)}, f32[8,1152]{1,0:T(8,128)}, bf16[1152,768]{1,0:T(8,128)(2,1)}, bf16[768,1152]{...) conditional(s32[]{:T(128)} %bitcast.3, ...), branch_computations={%region_0.0_spmd, %region_1.0_spmd, %region_2.0_spmd, %region_3.0_... | conditional | bytes 8 | solution.py:851
  16.5 196.4 %branch_0_fun.1 = (bf16[512,1152]{1,0:T(8,128)(2,1)}, f32[512,1152]{1,0:T(8,128)}, f32[8,1152]{1,0:T(8,128)}, bf16[1152,768]{1,0:T(8,128)(2,1)}, bf16[768,1152]{...) custom-call(bf16[512,1152]{1,0:T(8,128)(2,1)} %get-tuple-element.90.x_hbm, ...), custom_call_target="tpu_custom_call" | custom-call | tf_op jit(solution)/shard_map/cond/branch_0_fun/pallas_call | solution.py:851
  213.4 7.6 %shard_map.119 = (bf16[512,1152]{1,0:T(8,128)(2,1)}, f32[512,1152]{1,0:T(8,128)}, f32[9,128]{1,0:T(8,128)}, f32[4,1152]{1,0:T(4,128)}, f32[1152,768]{1,0:T(8,128)}, /*index=5*/f32[768,1152]{1,0:T(8,128)}) custom-call(bf16[512,1152]{1,0:T(8,128)(2,1)} %get-tuple-element.162.act, f32[512,1152]{1,0:T(8,128)} %get-tuple-element.163.ig, ...), custom_call_target="tpu_custom_call" | custom-call | tf_op jit(solution)/shard_map/pallas_call | solution.py:875
Async XLA Ops:
  0.6 15.8 %copy-start = (bf16[1,1152,768]{2,1,0:T(8,128)(2,1)S(1)}, bf16[1,1152,768]{2,1,0:T(8,128)(2,1)}, u32[]{:S(2)}) copy-start(bf16[1,1152,768]{2,1,0:T(8,128)(2,1)} %param.16) | copy-start | bytes 5308420
